TPU v7x, 128 devices: a whole 4x4x4 slice. The times are simulated.
128 devices in a mesh: row: 8 (over y, core), col: 16 (over z, x).
Axes of the slice: x: 4, y: 4, z: 4, core: 2. Of those that a mesh axis runs over, the one named last changes fastest.
Arguments:
- basis_values: bfloat16 [128, 1024, 2048], P(('row', 'col')), may hold values from -6 to 6
- grid_weights: float32 [128, 1024], P(('row', 'col')), may hold values from 0.005 to 0.1
- density_tiles: bfloat16 [16384, 128, 128], P(('row', 'col')), may hold values from -0.125 to 0.125
- tile_index: int32 [128, 256], P(('row', 'col')), may hold values from 0 to 16383, as said below
Outputs:
- potential_tiles: float32 [16384, 128, 128], P(('row', 'col'))
- grid_density: float32 [128, 1024], P(('row', 'col'))
Inputs may be any that keep to these rules, and one draw needn't show every extreme that they name: `tile_index`: within one region the 256 entries are distinct. An entry divided by 128 (rounded down) is the index, rows major, of the device storing that tile. One region names at most 4 tiles stored on one device, and one device is named exactly 4 times by every region.
All inputs are finite; a program needn't handle non-finite values.
Results may differ from a plain program's by a relative error of at most 0.0041.
Values may be sent and summed in bfloat16 or wider, within the bound.
No kernel may reach another device: no remote copies, remote signals or barrier semaphores. Data moves between devices by JAX's collectives and lax.ppermute only.
A program may use at most 128 MiB of HBM per device.

v0:
```python
import jax
import jax.numpy as jnp
from jax import lax
from jax.sharding import PartitionSpec as P

exchange_coeff = 0.9847450218426964


def per_device(basis_values, grid_weights, density_tiles, tile_index):
    rows_count = lax.axis_size("row")
    cols_count = lax.axis_size("col")
    devices = rows_count * cols_count
    stored = density_tiles.shape[0]
    width = density_tiles.shape[1]
    pairs = tile_index.shape[1]
    sig_count = basis_values.shape[2] // width
    points = basis_values.shape[1]
    capacity = 2 * pairs // devices
    slot_total = devices * capacity
    wanted = tile_index[0]
    owner_of = wanted // stored
    local_of = wanted % stored
    order_ids = jnp.arange(pairs, dtype=jnp.int32)
    earlier = order_ids[:, None] < order_ids[None, :]
    same_owner = owner_of[:, None] == owner_of[None, :]
    position = jnp.sum((same_owner & earlier).astype(jnp.int32), axis=0)
    slot_of = owner_of * capacity + position
    slot_ids = jnp.arange(slot_total, dtype=jnp.int32)
    matches = (slot_of[None, :] == slot_ids[:, None]).astype(jnp.int32)
    filled = jnp.sum(matches, axis=1) > 0
    pair_of_slot = jnp.sum(matches * order_ids[None, :], axis=1)
    send_local = jnp.where(filled, jnp.sum(matches * local_of[None, :], axis=1), -1)
    asked = lax.all_to_all(send_local, ("row", "col"), split_axis=0, concat_axis=0, tiled=True)
    asked_valid = asked >= 0
    fetched = density_tiles[jnp.maximum(asked, 0)]
    fetched = jnp.where(asked_valid[:, None, None], fetched, jnp.zeros_like(fetched))
    reply = lax.all_to_all(fetched, ("row", "col"), split_axis=0, concat_axis=0, tiled=True)
    block_tiles = reply[slot_of].reshape(sig_count, sig_count, width, width)
    values = basis_values[0].reshape(points, sig_count, width)
    mixed = jnp.einsum("npi,pqij->nqj", values, block_tiles, preferred_element_type=jnp.float32)
    density = jnp.sum(mixed * values, axis=(1, 2))
    weighted = (
        -exchange_coeff * grid_weights[0] * density / (density * density + 1.0) ** (1.0 / 3.0)
    )
    scaled = (weighted[:, None, None] * values).astype(jnp.bfloat16)
    partial_tiles = jnp.einsum("npi,nqj->pqij", values, scaled, preferred_element_type=jnp.float32)
    partial_tiles = partial_tiles.astype(jnp.bfloat16).reshape(pairs, width, width)
    outgoing = partial_tiles[pair_of_slot]
    outgoing = jnp.where(filled[:, None, None], outgoing, jnp.zeros_like(outgoing))
    arrived = lax.all_to_all(outgoing, ("row", "col"), split_axis=0, concat_axis=0, tiled=True)
    selector = (asked[None, :] == jnp.arange(stored, dtype=jnp.int32)[:, None]).astype(jnp.bfloat16)
    summed = jnp.dot(
        selector, arrived.reshape(slot_total, width * width), preferred_element_type=jnp.float32
    )
    return (summed.reshape(stored, width, width), density[None, :])


def solution(mesh):
    in_specs = (
        P(("row", "col"), None, None),
        P(("row", "col"), None),
        P(("row", "col"), None, None),
        P(("row", "col"), None),
    )
    out_specs = (P(("row", "col"), None, None), P(("row", "col"), None))
    return jax.shard_map(
        per_device, mesh=mesh, in_specs=in_specs, out_specs=out_specs, check_vma=False
    )
```

profile of v0, /device:TPU:1, one launch (start us, length us, event | category | flops | bytes accessed | tf_op | source)
XLA Modules:
  0.0 642.1 jit_solution(9371853795852017311)
XLA Ops:
  0.6 0.7 and_select_fusion.1
  1.3 0.7 and_select_fusion.2
  2.0 0.7 and_select_fusion.3
  2.7 0.1 convert_reduce_fusion.1
  2.8 0.3 select_reduce_fusion
  3.2 0.1 select_n.75
  3.3 21.1 %all_to_all.16 = s32[128,4,1]{1,2,0:T(1,128)S(1)} all-to-all(s32[128,4,1]{1,2,0:T(1,128)S(1)} %bitcast.64), channel_id=1, replica_groups=mesh['row'=8,'col'=16] {'row','col'}, dimensions={0} | all-to-all | bytes 4096 | tf_op jit(solution)/shard_map/all_to_all | solution.py:33
  24.4 0.5 broadcast.242
  24.9 1.0 fusion.7
  25.9 0.1 eq.55
  26.0 0.1 reshape.195
  26.1 15.6 %gather_fusion = bf16[512,128,128]{2,1,0:T(8,128)(2,1)} fusion(bf16[128,128,128]{2,1,0:T(8,128)(2,1)} %param.6, s32[1024]{0:T(1024)S(1)} %pad_clamp_fusion.2), kind=kCustom, calls=%fused_computation | custom fusion | bytes 33556480 | tf_op jit(solution)/shard_map/gather | solution.py:35
  41.7 14.4 %broadcast_select_fusion = bf16[512,128,128]{2,1,0:T(8,128)(2,1)} fusion(bf16[512,128,128]{2,1,0:T(8,128)(2,1)} %gather_fusion, pred[512]{0:T(512)(128)(4,1)S(1)} %broadcast_compare_fusion), kind=kLoop, calls=%fused_computation.5 | loop fusion | flops 8388608 | bytes 33554944 | tf_op jit(solution)/shard_map/jit(_where)/select_n | solution.py:36
  56.1 5.5 all-to-all-start.1
  61.6 0.0 copy-start.1
  61.6 0.0 copy-start.3
  61.6 6.4 %copy.31 = bf16[1,1024,2048]{1,2,0:T(8,128)(2,1)} copy(bf16[1,1024,2048]{2,1,0:T(8,128)(2,1)} %param.4) | data formatting | bytes 8388608 | tf_op args[0]
  68.1 0.0 copy-done.3
  68.1 227.5 %all-to-all-done.1 = bf16[512,128,128]{2,1,0:T(8,128)(2,1)} async-done(((bf16[512,128,128]{2,1,0:T(8,128)(2,1)}), bf16[512,128,128]{2,1,0:T(8,128)(2,1)}, u32[]{:S(2)}, u32[]{:S(2)}) %all-to-all-start.1) | async-done | bytes 16777248 | tf_op jit(solution)/shard_map/all_to_all | solution.py:37
  295.6 14.6 %gather_fusion.1 = bf16[256,128,128]{2,1,0:T(8,128)(2,1)} fusion(bf16[512,128,128]{2,1,0:T(8,128)(2,1)} %all-to-all-done.1, s32[1024]{0:T(1024)S(1)} %pad_clamp_fusion.1), kind=kCustom, calls=%fused_computation.1 | custom fusion | bytes 16778240 | tf_op jit(solution)/shard_map/gather | solution.py:38
  310.2 14.8 %fusion.2 = f32[1024]{0:T(1024)S(1)} fusion(bf16[1024,16,128]{0,2,1:T(8,128)(2,1)} %bitcast.60, bf16[16,16,128,128]{3,2,1,0:T(8,128)(2,1)} %bitcast.59, bf16[1024,16,128,1]{0,2,3,1:T(8,128)(2,1)} %bitcast.61), kind=kOutput, calls=%fused_computation.8 | convolution fusion | flops 8596225024 | bytes 16781312 | tf_op jit(solution)/shard_map/npi,pqij->nqj/dot_general | solution.py:40
  325.0 0.0 copy-start.2
  325.1 2.8 multiply_convert_fusion
  327.8 6.4 copy.45
  334.2 13.4 %convert_bitcast_fusion = bf16[16,16,128,128]{2,3,0,1:T(8,128)(2,1)} fusion(bf16[1024,16,128,1]{0,2,3,1:T(8,128)(2,1)} %bitcast.63, bf16[1024,16,128,1]{0,2,1,3:T(8,128)(2,1)} %bitcast.62), kind=kOutput, calls=%fused_computation.9 | convolution fusion | flops 8594128896 | bytes 16777216 | tf_op jit(solution)/shard_map/npi,nqj->pqij/dot_general | solution.py:46
  347.6 12.3 %copy.36 = bf16[16,16,128,128]{3,2,1,0:T(8,128)(2,1)} copy(bf16[16,16,128,128]{2,3,0,1:T(8,128)(2,1)} %convert_bitcast_fusion) | data formatting | bytes 16777216 | tf_op jit(solution)/shard_map/convert_element_type | solution.py:47
  359.9 17.1 %gather_fusion.2 = bf16[512,128,128]{2,1,0:T(8,128)(2,1)} fusion(bf16[256,128,128]{2,1,0:T(8,128)(2,1)} %bitcast.58, s32[1024]{0:T(1024)S(1)} %pad_clamp_fusion), kind=kCustom, calls=%fused_computation.2 | custom fusion | bytes 33556480 | tf_op jit(solution)/shard_map/gather | solution.py:48
  377.0 8.8 %broadcast_select_fusion.1 = bf16[512,128,128]{2,1,0:T(8,128)(2,1)S(1)} fusion(bf16[512,128,128]{2,1,0:T(8,128)(2,1)} %gather_fusion.2, pred[512]{0:T(512)(128)(4,1)S(1)} %get-tuple-element.16), kind=kLoop, calls=%fused_computation.6 | loop fusion | flops 8388608 | bytes 33554944 | tf_op jit(solution)/shard_map/jit(_where)/select_n | solution.py:49
  385.9 205.8 %all_to_all.17 = bf16[512,128,128]{2,1,0:T(8,128)(2,1)} all-to-all(bf16[512,128,128]{2,1,0:T(8,128)(2,1)S(1)} %broadcast_select_fusion.1), channel_id=1, replica_groups=mesh['row'=8,'col'=16] {'row','col'}, dimensions={0} | all-to-all | bytes 33554432 | tf_op jit(solution)/shard_map/all_to_all | solution.py:50
  591.6 24.3 %copy.47 = bf16[512,128,128]{0,2,1:T(8,128)(2,1)} copy(bf16[512,128,128]{2,1,0:T(8,128)(2,1)} %all_to_all.17) | data formatting | bytes 33554432 | tf_op jit(solution)/shard_map/reshape | solution.py:53
  616.0 14.5 %fusion = f32[128,128,128]{2,0,1:T(8,128)} fusion(bf16[512,128,128]{0,2,1:T(8,128)(2,1)} %copy.47, s32[512]{0:T(512)S(1)} %eq.55), kind=kOutput, calls=%fused_computation.3 | convolution fusion | flops 2147549184 | bytes 25167872 | tf_op jit(solution)/shard_map/dot_general | solution.py:52
  630.5 11.6 %copy.38 = f32[128,128,128]{2,1,0:T(8,128)} copy(f32[128,128,128]{2,0,1:T(8,128)} %fusion) | data formatting | bytes 16777216
  (14 shorter events, 0.1 us)
Async XLA Ops:
  56.1 239.6 %all-to-all-start.1 = ((bf16[512,128,128]{2,1,0:T(8,128)(2,1)}), bf16[512,128,128]{2,1,0:T(8,128)(2,1)}, u32[]{:S(2)}, u32[]{:S(2)}) async-start(bf16[512,128,128]{2,1,0:T(8,128)(2,1)} %broadcast_select_fusion), calls=%async_computation.1 | async-start | bytes 33554432 | tf_op jit(solution)/shard_map/all_to_all | solution.py:37
  61.6 6.5 %copy-start.1 = (s32[1,256]{1,0:T(1,128)S(1)}, s32[1,256]{1,0:T(1,128)}, u32[]{:S(2)}) copy-start(s32[1,256]{1,0:T(1,128)} %param.7) | copy-start | bytes 3076
  61.6 6.5 %copy-start.3 = (f32[1,1024]{1,0:T(1,128)S(1)}, f32[1,1024]{1,0:T(1,128)}, u32[]{:S(2)}) copy-start(f32[1,1024]{1,0:T(1,128)} %param.5) | copy-start | bytes 12292
  310.2 14.9 %copy-start = (bf16[1,1024,2048]{2,1,0:T(8,128)(2,1)S(1)}, bf16[1,1024,2048]{2,1,0:T(8,128)(2,1)}, u32[]{:S(2)}) copy-start(bf16[1,1024,2048]{2,1,0:T(8,128)(2,1)} %param.4) | copy-start | bytes 12582916
  325.0 9.2 %copy-start.2 = (f32[1024]{0:T(1024)}, f32[1024]{0:T(1024)S(1)}, u32[]{:S(2)}) copy-start(f32[1024]{0:T(1024)S(1)} %fusion.2) | copy-start | bytes 12292
where the time goes:
time: 644 us; the launch traced here: 642 us
  blocking collectives  227 us (35%)
  waiting for transfers between devices  227 us (35%)
  local copies, waits for them, and re-layouts  109 us (17%)
  matrix products  42.8 us (7%)
  other arithmetic  29.6 us (5%)
    all_to_all x1, waiting for transfers between devices, per_device(): lax.all_to_all(fetched, ('row', 'col'), split_axis=0, concat_axis=0, tile...  227 us
    all_to_all x1, blocking collectives, per_device(): lax.all_to_all(outgoing, ('row', 'col'), split_axis=0, concat_axis=0, til...  206 us
    reshape x1, local copies, waits for them, and re-layouts, per_device(): arrived.reshape(slot_total, width * width)  24.3 us
    all_to_all x1, blocking collectives, per_device(): lax.all_to_all(send_local, ('row', 'col'), split_axis=0, concat_axis=0, t...  21.1 us
    unnamed x10, local copies, waits for them, and re-layouts  18.1 us
    gather x1, local copies, waits for them, and re-layouts, per_device(): outgoing = partial_tiles[pair_of_slot]  17.1 us
    gather x1, local copies, waits for them, and re-layouts, per_device(): fetched = density_tiles[jnp.maximum(asked, 0)]  15.6 us
    dot_general x1, matrix products, per_device(): jnp.einsum('npi,pqij->nqj', values, block_tiles, preferred_element_type=j...  14.8 us
  transfers between devices with their start and end apart: 1, of which 1 were waited for; matrix products, arithmetic and copies ran while one was open for 1% of the time, Pallas kernels for 0%

commit v1 on v0

v1 whole, which is shorter than its diff:
```python
import functools

import jax
import jax.numpy as jnp
from jax import lax
from jax.experimental import pallas as pl
from jax.experimental.pallas import tpu as pltpu
from jax.sharding import PartitionSpec as P

exchange_coeff = 0.9847450218426964
AXES = ("row", "col")
VMEM_BYTES = 56 * 1024 * 1024


def fetch_kernel(asked_ref, tiles_ref, out_ref, sem):
    slots = out_ref.shape[0]

    def start(step, carry):
        for lane in range(8):
            slot = step * 8 + lane
            tile = jnp.maximum(asked_ref[slot], 0)
            pltpu.make_async_copy(tiles_ref.at[tile], out_ref.at[slot], sem).start()
        return carry

    lax.fori_loop(0, slots // 8, start, 0)
    pltpu.make_async_copy(out_ref, out_ref, sem).wait()


def region_kernel(
    slot_ref, values_ref, turned_ref, weights_ref, reply_ref, out_ref, density_ref,
    block, scaled, partial, load_sems, store_sem,
):
    points, width_all = values_ref.shape
    width = reply_ref.shape[1]
    sig = width_all // width
    chunk = 2 * width
    chunks = width_all // chunk

    def start_chunk(j):
        def body(p, carry):
            for half in range(2):
                q = 2 * j + half
                slot = slot_ref[p * sig + q]
                pltpu.make_async_copy(
                    reply_ref.at[slot],
                    block.at[pl.ds(pl.multiple_of(p * width, width), width), pl.ds(q * width, width)],
                    load_sems.at[j],
                ).start()
            return carry

        lax.fori_loop(0, sig, body, 0)

    for j in range(chunks):
        start_chunk(j)
    total = jnp.zeros((points, width), jnp.float32)
    for j in range(chunks):
        columns = block.at[:, pl.ds(j * chunk, chunk)]
        pltpu.make_async_copy(columns, columns, load_sems.at[j]).wait()
        mixed = jnp.dot(values_ref[...], columns[...], preferred_element_type=jnp.float32)
        product = mixed * values_ref[:, pl.ds(j * chunk, chunk)].astype(jnp.float32)
        total = total + product[:, :width] + product[:, width:]
    density = jnp.sum(total, axis=1, keepdims=True)
    density = jnp.broadcast_to(density, (points, width))
    density_ref[...] = density.T[:1, :]
    weights = jnp.broadcast_to(weights_ref[...], (width, points)).T
    cube_root = jnp.exp(jnp.log(density * density + 1.0) * (1.0 / 3.0))
    weighted = -exchange_coeff * weights * density / cube_root
    for q in range(sig):
        columns = pl.ds(q * width, width)
        scaled[:, columns] = (weighted * values_ref[:, columns].astype(jnp.float32)).astype(jnp.bfloat16)
    for i in range(chunks):
        rows = pl.ds(i * chunk, chunk)
        partial[rows, :] = jnp.dot(
            turned_ref[rows, :], scaled[...], preferred_element_type=jnp.float32
        ).astype(jnp.bfloat16)

        def store(q, carry):
            for half in range(2):
                p = 2 * i + half
                pltpu.make_async_copy(
                    partial.at[pl.ds(p * width, width), pl.ds(pl.multiple_of(q * width, width), width)],
                    out_ref.at[slot_ref[p * sig + q]],
                    store_sem,
                ).start()
            return carry

        lax.fori_loop(0, sig, store, 0)
    pltpu.make_async_copy(partial, partial, store_sem).wait()


def collect_kernel(asked_ref, arrived_ref, out_ref, held, sems):
    slots = arrived_ref.shape[0]
    parts = sems.shape[0]
    size = slots // parts

    def piece(j):
        return pltpu.make_async_copy(
            arrived_ref.at[pl.ds(j * size, size)], held.at[pl.ds(j * size, size)], sems.at[j]
        )

    for j in range(parts):
        piece(j).start()
    out_ref[...] = jnp.zeros_like(out_ref)

    def add(slot, carry):
        tile = asked_ref[slot]

        @pl.when(tile >= 0)
        def _():
            out_ref[tile] = out_ref[tile] + held[slot].astype(jnp.float32)

        return carry

    for j in range(parts):
        piece(j).wait()
        lax.fori_loop(j * size, (j + 1) * size, add, 0)


def fetch(asked, tiles):
    slots = asked.shape[0]
    return pl.pallas_call(
        fetch_kernel,
        out_shape=jax.ShapeDtypeStruct((slots,) + tiles.shape[1:], tiles.dtype),
        in_specs=[pl.BlockSpec(memory_space=pltpu.SMEM), pl.BlockSpec(memory_space=pltpu.VMEM)],
        out_specs=pl.BlockSpec(memory_space=pl.ANY),
        scratch_shapes=[pltpu.SemaphoreType.DMA],
        compiler_params=pltpu.CompilerParams(vmem_limit_bytes=VMEM_BYTES),
        name="fetch_tiles",
    )(asked, tiles)


def region(slot_of, values, turned, weights, reply):
    points, width_all = values.shape
    width = reply.shape[1]
    chunks = width_all // (2 * width)
    vmem = pl.BlockSpec(memory_space=pltpu.VMEM)
    hbm = pl.BlockSpec(memory_space=pl.ANY)
    return pl.pallas_call(
        region_kernel,
        out_shape=(
            jax.ShapeDtypeStruct(reply.shape, jnp.bfloat16),
            jax.ShapeDtypeStruct((1, points), jnp.float32),
        ),
        in_specs=[pl.BlockSpec(memory_space=pltpu.SMEM), vmem, vmem, vmem, hbm],
        out_specs=(hbm, vmem),
        scratch_shapes=[
            pltpu.VMEM((width_all, width_all), jnp.bfloat16),
            pltpu.VMEM((points, width_all), jnp.bfloat16),
            pltpu.VMEM((width_all, width_all), jnp.bfloat16),
            pltpu.SemaphoreType.DMA((chunks,)),
            pltpu.SemaphoreType.DMA,
        ],
        compiler_params=pltpu.CompilerParams(vmem_limit_bytes=VMEM_BYTES),
        name="region_work",
    )(slot_of, values, turned, weights, reply)


def collect(asked, arrived, stored):
    return pl.pallas_call(
        collect_kernel,
        out_shape=jax.ShapeDtypeStruct((stored,) + arrived.shape[1:], jnp.float32),
        in_specs=[pl.BlockSpec(memory_space=pltpu.SMEM), pl.BlockSpec(memory_space=pl.ANY)],
        out_specs=pl.BlockSpec(memory_space=pltpu.VMEM),
        scratch_shapes=[
            pltpu.VMEM(arrived.shape, jnp.bfloat16),
            pltpu.SemaphoreType.DMA((8,)),
        ],
        compiler_params=pltpu.CompilerParams(vmem_limit_bytes=VMEM_BYTES),
        name="collect_tiles",
    )(asked, arrived)


def per_device(basis_values, grid_weights, density_tiles, tile_index):
    devices = lax.axis_size("row") * lax.axis_size("col")
    stored = density_tiles.shape[0]
    pairs = tile_index.shape[1]
    capacity = 2 * pairs // devices
    slot_total = devices * capacity
    exchange = functools.partial(
        lax.all_to_all, axis_name=AXES, split_axis=0, concat_axis=0, tiled=True
    )
    wanted = tile_index[0]
    owner_of = wanted // stored
    local_of = wanted % stored
    order_ids = jnp.arange(pairs, dtype=jnp.int32)
    earlier = order_ids[:, None] < order_ids[None, :]
    same_owner = owner_of[:, None] == owner_of[None, :]
    position = jnp.sum((same_owner & earlier).astype(jnp.int32), axis=0)
    slot_of = owner_of * capacity + position
    slot_ids = jnp.arange(slot_total, dtype=jnp.int32)
    matches = (slot_of[None, :] == slot_ids[:, None]).astype(jnp.int32)
    send_local = jnp.sum(matches * (local_of + 1)[None, :], axis=1) - 1
    asked = exchange(send_local)
    reply = exchange(fetch(asked, density_tiles))
    values = basis_values[0]
    outgoing, density = region(slot_of, values, values.T, grid_weights, reply)
    arrived = exchange(outgoing)
    return collect(asked, arrived, stored), density


def solution(mesh):
    in_specs = (
        P(AXES, None, None),
        P(AXES, None),
        P(AXES, None, None),
        P(AXES, None),
    )
    out_specs = (P(AXES, None, None), P(AXES, None))
    return jax.shard_map(
        per_device, mesh=mesh, in_specs=in_specs, out_specs=out_specs, check_vma=False
    )
```

time: 644 us -> 531 us (0.82)
  local copies, waits for them, and re-layouts: 109 us -> 7.72 us
  Pallas kernels: 0 us -> 58.2 us
  matrix products: 42.8 us -> 0 us
  other arithmetic: 29.6 us -> 3.05 us
    pallas_call x0 -> x3, Pallas kernels: none -> 58.2 us  [the longest x1 36.6 us: region(): pl.pallas_call(region_kernel, out_shape=(jax.ShapeDtypeStruct(reply.shape...]
    gather x3 -> x0, local copies, waits for them, and re-layouts: 47.2 us -> none  [the longest x1 17.1 us: per_device(): outgoing = partial_tiles[pair_of_slot]]
    dot_general x3 -> x0, matrix products: 42.8 us -> none  [the longest x1 14.8 us: per_device(): jnp.einsum('npi,pqij->nqj', values, block_tiles, preferred_element_type=j...]
    reshape x1 -> x0, local copies, waits for them, and re-layouts: 24.3 us -> none  [per_device(): arrived.reshape(slot_total, width * width)]
    select_n x6 -> x0, other arithmetic: 23.9 us -> none  [the longest x1 14.4 us: per_device(): jnp.where(asked_valid[:, None, None], fetched, jnp.zeros_like(fetched))]
    convert_element_type x2 -> x0, local copies, waits for them, and re-layouts: 18.7 us -> none  [the longest x1 12.3 us: per_device(): partial_tiles.astype(jnp.bfloat16).reshape(pairs, width, width)]
    unnamed x10 -> x3, local copies, waits for them, and re-layouts: 18.1 us -> 6.41 us
where the time goes in v1:
time: 531 us; the launch traced here: 530 us
  blocking collectives  229 us (43%)
  waiting for transfers between devices  226 us (43%)
  Pallas kernels  58.2 us (11%)
  local copies, waits for them, and re-layouts  7.72 us (1%)
  starting transfers between devices  5.52 us (1%)
    all_to_all x1, waiting for transfers between devices, per_device(): reply = exchange(fetch(asked, density_tiles))  226 us
    all_to_all x1, blocking collectives, per_device(): arrived = exchange(outgoing)  208 us
    pallas_call x1, Pallas kernels, region(): pl.pallas_call(region_kernel, out_shape=(jax.ShapeDtypeStruct(reply.shape...  36.6 us
    all_to_all x1, blocking collectives, per_device(): asked = exchange(send_local)  21.1 us
    pallas_call x1, Pallas kernels, collect(): pl.pallas_call(collect_kernel, out_shape=jax.ShapeDtypeStruct((stored,) +...  13.7 us
  transfers between devices with their start and end apart: 1, of which 1 were waited for; matrix products, arithmetic and copies ran while one was open for 1% of the time, Pallas kernels for 0%

profile of v1, /device:TPU:1, one launch (start us, length us, event | category | flops | bytes accessed | tf_op | source)
XLA Modules:
  0.0 530.3 jit_solution(13064181226290833839)
XLA Ops:
  0.6 0.7 and_select_fusion.1
  1.3 0.7 and_select_fusion.2
  2.0 0.1 convert_reduce_fusion
  2.1 0.2 select_reduce_fusion
  2.3 0.1 sub.17
  2.4 21.1 %all_to_all.18 = s32[128,4,1]{1,2,0:T(1,128)S(1)} all-to-all(s32[128,4,1]{1,2,0:T(1,128)S(1)} %bitcast.13), channel_id=1, replica_groups=mesh['row'=8,'col'=16] {'row','col'}, dimensions={0} | all-to-all | bytes 4096 | tf_op jit(solution)/shard_map/all_to_all | solution.py:193
  23.5 0.5 broadcast.99
  24.0 0.8 reduce.3
  24.8 0.7 all_to_all.12.asked_ref
  25.5 7.9 %fetch_tiles.1 = bf16[512,128,128]{2,1,0:T(8,128)(2,1)} custom-call(s32[512]{0:T(512)} %all_to_all.12.asked_ref, bf16[128,128,128]{2,1,0:T(8,128)(2,1)} %tiles_ref.1), custom_call_target="tpu_custom_call" | custom-call | tf_op jit(solution)/shard_map/fetch_tiles/pallas_call | solution.py:121
  33.5 0.0 copy-start
  33.5 5.5 %all-to-all-start.1 = ((bf16[512,128,128]{2,1,0:T(8,128)(2,1)}), bf16[512,128,128]{2,1,0:T(8,128)(2,1)}, u32[]{:S(2)}, u32[]{:S(2)}) async-start(bf16[512,128,128]{2,1,0:T(8,128)(2,1)} %fetch_tiles.1), calls=%async_computation.1 | async-start | bytes 33554432 | tf_op jit(solution)/shard_map/all_to_all | solution.py:194
  39.0 6.4 %copy.14 = bf16[1,1024,2048]{1,2,0:T(8,128)(2,1)} copy(bf16[1,1024,2048]{2,1,0:T(8,128)(2,1)} %param.4) | data formatting | bytes 8388608 | tf_op args[0]
  45.4 0.0 copy-done
  45.4 0.6 multiply_add_fusion.slot_ref
  46.0 225.6 %all-to-all-done.1.reply_ref = bf16[512,128,128]{2,1,0:T(8,128)(2,1)} async-done(((bf16[512,128,128]{2,1,0:T(8,128)(2,1)}), bf16[512,128,128]{2,1,0:T(8,128)(2,1)}, u32[]{:S(2)}, u32[]{:S(2)}) %all-to-all-start.1) | async-done | bytes 16777248 | tf_op jit(solution)/shard_map/all_to_all | solution.py:194
  271.6 36.6 %region_work.1 = (bf16[512,128,128]{2,1,0:T(8,128)(2,1)}, f32[1,1024]{1,0:T(1,128)}) custom-call(s32[256]{0:T(256)} %multiply_add_fusion.slot_ref, bf16[1024,2048]{1,0:T(8,128)(2,1)} %bitcast.11, bf16[2048,1024]{1,0:T(8,128)(2,1)} %bitcast.12, f32[1,1024]{1,0:T(1,128)} %weights_ref.1, bf16[512,128,128]{2,1,0:T(8,128)(2,1)} %all-to-all-done.1.reply_ref), custom_call_target="tpu_custom_call" | custom-call | tf_op jit(solution)/shard_map/region_work/pallas_call | solution.py:138
  308.2 208.3 %all_to_all.19.arrived_ref = bf16[512,128,128]{2,1,0:T(8,128)(2,1)} all-to-all(bf16[512,128,128]{2,1,0:T(8,128)(2,1)} %get-tuple-element.4), channel_id=1, replica_groups=mesh['row'=8,'col'=16] {'row','col'}, dimensions={0} | all-to-all | bytes 33554432 | tf_op jit(solution)/shard_map/all_to_all | solution.py:197
  516.4 13.7 %collect_tiles.1 = f32[128,128,128]{2,1,0:T(8,128)} custom-call(s32[512]{0:T(512)} %all_to_all.12.asked_ref, bf16[512,128,128]{2,1,0:T(8,128)(2,1)} %all_to_all.19.arrived_ref), custom_call_target="tpu_custom_call" | custom-call | tf_op jit(solution)/shard_map/collect_tiles/pallas_call | solution.py:159
  (2 shorter events, 0.0 us)
Async XLA Ops:
  33.5 11.9 %copy-start = (s32[1,256]{1,0:T(1,128)S(1)}, s32[1,256]{1,0:T(1,128)}, u32[]{:S(2)}) copy-start(s32[1,256]{1,0:T(1,128)} %param.7) | copy-start | bytes 3076
  33.5 238.1 %all-to-all-start.1 = ((bf16[512,128,128]{2,1,0:T(8,128)(2,1)}), bf16[512,128,128]{2,1,0:T(8,128)(2,1)}, u32[]{:S(2)}, u32[]{:S(2)}) async-start(bf16[512,128,128]{2,1,0:T(8,128)(2,1)} %fetch_tiles.1), calls=%async_computation.1 | async-start | bytes 33554432 | tf_op jit(solution)/shard_map/all_to_all | solution.py:194

commit v2 on v1

--- a/solution.py
+++ b/solution.py
@@ -27,38 +27,35 @@
 
 
 def region_kernel(
-    slot_ref, values_ref, turned_ref, weights_ref, reply_ref, out_ref, density_ref,
+    slot_ref, values_ref, weights_ref, reply_ref, out_ref, density_ref,
     block, scaled, partial, load_sems, store_sem,
 ):
     points, width_all = values_ref.shape
     width = reply_ref.shape[1]
     sig = width_all // width
-    chunk = 2 * width
+    chunk = 4 * width
     chunks = width_all // chunk
 
     def start_chunk(j):
-        def body(p, carry):
-            for half in range(2):
-                q = 2 * j + half
-                slot = slot_ref[p * sig + q]
+        for q in range(4 * j, 4 * j + 4):
+            for p in range(sig):
                 pltpu.make_async_copy(
-                    reply_ref.at[slot],
-                    block.at[pl.ds(pl.multiple_of(p * width, width), width), pl.ds(q * width, width)],
-                    load_sems.at[j],
+                    reply_ref.at[slot_ref[p * sig + q]], block.at[q, pl.ds(p * width, width)], load_sems.at[j]
                 ).start()
-            return carry
-
-        lax.fori_loop(0, sig, body, 0)
-
-    for j in range(chunks):
+
+    ahead = 2
+    for j in range(ahead):
         start_chunk(j)
     total = jnp.zeros((points, width), jnp.float32)
     for j in range(chunks):
-        columns = block.at[:, pl.ds(j * chunk, chunk)]
-        pltpu.make_async_copy(columns, columns, load_sems.at[j]).wait()
-        mixed = jnp.dot(values_ref[...], columns[...], preferred_element_type=jnp.float32)
+        if j + ahead < chunks:
+            start_chunk(j + ahead)
+        pair = block.at[pl.ds(4 * j, 4)]
+        pltpu.make_async_copy(pair, pair, load_sems.at[j]).wait()
+        columns = jnp.concatenate([block[4 * j + k] for k in range(4)], axis=1)
+        mixed = jnp.dot(values_ref[...], columns, preferred_element_type=jnp.float32)
         product = mixed * values_ref[:, pl.ds(j * chunk, chunk)].astype(jnp.float32)
-        total = total + product[:, :width] + product[:, width:]
+        total = total + sum(product[:, k * width:(k + 1) * width] for k in range(4))
     density = jnp.sum(total, axis=1, keepdims=True)
     density = jnp.broadcast_to(density, (points, width))
     density_ref[...] = density.T[:1, :]
@@ -70,21 +67,14 @@
         scaled[:, columns] = (weighted * values_ref[:, columns].astype(jnp.float32)).astype(jnp.bfloat16)
     for i in range(chunks):
         rows = pl.ds(i * chunk, chunk)
-        partial[rows, :] = jnp.dot(
-            turned_ref[rows, :], scaled[...], preferred_element_type=jnp.float32
+        result = lax.dot_general(
+            values_ref[:, rows], scaled[...], (((0,), (0,)), ((), ())), preferred_element_type=jnp.float32
         ).astype(jnp.bfloat16)
-
-        def store(q, carry):
-            for half in range(2):
-                p = 2 * i + half
-                pltpu.make_async_copy(
-                    partial.at[pl.ds(p * width, width), pl.ds(pl.multiple_of(q * width, width), width)],
-                    out_ref.at[slot_ref[p * sig + q]],
-                    store_sem,
-                ).start()
-            return carry
-
-        lax.fori_loop(0, sig, store, 0)
+        for half in range(4):
+            for q in range(sig):
+                pair = (4 * i + half) * sig + q
+                partial[pair] = result[half * width:(half + 1) * width, q * width:(q + 1) * width]
+                pltpu.make_async_copy(partial.at[pair], out_ref.at[slot_ref[pair]], store_sem).start()
     pltpu.make_async_copy(partial, partial, store_sem).wait()
 
 
@@ -129,10 +119,10 @@
     )(asked, tiles)
 
 
-def region(slot_of, values, turned, weights, reply):
+def region(slot_of, values, weights, reply):
     points, width_all = values.shape
     width = reply.shape[1]
-    chunks = width_all // (2 * width)
+    chunks = width_all // (4 * width)
     vmem = pl.BlockSpec(memory_space=pltpu.VMEM)
     hbm = pl.BlockSpec(memory_space=pl.ANY)
     return pl.pallas_call(
@@ -141,18 +131,18 @@
             jax.ShapeDtypeStruct(reply.shape, jnp.bfloat16),
             jax.ShapeDtypeStruct((1, points), jnp.float32),
         ),
-        in_specs=[pl.BlockSpec(memory_space=pltpu.SMEM), vmem, vmem, vmem, hbm],
+        in_specs=[pl.BlockSpec(memory_space=pltpu.SMEM), vmem, vmem, hbm],
         out_specs=(hbm, vmem),
         scratch_shapes=[
-            pltpu.VMEM((width_all, width_all), jnp.bfloat16),
+            pltpu.VMEM((width_all // width, width_all, width), jnp.bfloat16),
             pltpu.VMEM((points, width_all), jnp.bfloat16),
-            pltpu.VMEM((width_all, width_all), jnp.bfloat16),
+            pltpu.VMEM((slot_of.shape[0], width, width), jnp.bfloat16),
             pltpu.SemaphoreType.DMA((chunks,)),
             pltpu.SemaphoreType.DMA,
         ],
         compiler_params=pltpu.CompilerParams(vmem_limit_bytes=VMEM_BYTES),
         name="region_work",
-    )(slot_of, values, turned, weights, reply)
+    )(slot_of, values, weights, reply)
 
 
 def collect(asked, arrived, stored):
@@ -193,7 +183,7 @@
     asked = exchange(send_local)
     reply = exchange(fetch(asked, density_tiles))
     values = basis_values[0]
-    outgoing, density = region(slot_of, values, values.T, grid_weights, reply)
+    outgoing, density = region(slot_of, values, grid_weights, reply)
     arrived = exchange(outgoing)
     return collect(asked, arrived, stored), density
 

time: 531 us -> 519 us (0.977)
  Pallas kernels: 58.2 us -> 46 us
  local copies, waits for them, and re-layouts: 7.72 us -> 1.32 us
  waiting for transfers between devices: 226 us -> 232 us
    pallas_call x1, Pallas kernels: 36.6 us -> 24.6 us  [region(): pl.pallas_call(region_kernel, out_shape=(jax.ShapeDtypeStruct(reply.shape...]
    all_to_all x1, waiting for transfers between devices: 226 us -> 232 us  [per_device(): reply = exchange(fetch(asked, density_tiles))]
    unnamed x3 -> x2, local copies, waits for them, and re-layouts: 6.41 us -> 0.01 us
  transfers between devices with their start and end apart: 1 -> 1, of which waited for: 1 -> 1; matrix products, arithmetic and copies ran while one was open for 1% -> 0% of each run, Pallas kernels for 0% -> 0%
where the time goes in v2:
time: 519 us; the launch traced here: 518 us
  waiting for transfers between devices  232 us (45%)
  blocking collectives  229 us (44%)
  Pallas kernels  46 us (9%)
  starting transfers between devices  5.52 us (1%)
    all_to_all x1, waiting for transfers between devices, per_device(): reply = exchange(fetch(asked, density_tiles))  232 us
    all_to_all x1, blocking collectives, per_device(): arrived = exchange(outgoing)  208 us
    pallas_call x1, Pallas kernels, region(): pl.pallas_call(region_kernel, out_shape=(jax.ShapeDtypeStruct(reply.shape...  24.6 us
    all_to_all x1, blocking collectives, per_device(): asked = exchange(send_local)  21.1 us
    pallas_call x1, Pallas kernels, collect(): pl.pallas_call(collect_kernel, out_shape=jax.ShapeDtypeStruct((stored,) +...  13.5 us
  transfers between devices with their start and end apart: 1, of which 1 were waited for; matrix products, arithmetic and copies ran while one was open for 0% of the time, Pallas kernels for 0%

profile of v2, /device:TPU:1, one launch (start us, length us, event | category | flops | bytes accessed | tf_op | source)
XLA Modules:
  0.0 518.1 jit_solution(13153248284026141368)
XLA Ops:
  0.6 0.7 and_select_fusion.1
  1.3 0.7 and_select_fusion.2
  2.0 0.1 convert_reduce_fusion
  2.1 0.2 select_reduce_fusion
  2.3 0.1 sub.17
  2.4 21.1 %all_to_all.18 = s32[128,4,1]{1,2,0:T(1,128)S(1)} all-to-all(s32[128,4,1]{1,2,0:T(1,128)S(1)} %bitcast.9), channel_id=1, replica_groups=mesh['row'=8,'col'=16] {'row','col'}, dimensions={0} | all-to-all | bytes 4096 | tf_op jit(solution)/shard_map/all_to_all | solution.py:183
  23.5 0.5 broadcast.99
  24.0 0.8 reduce.3
  24.8 0.7 all_to_all.12.asked_ref
  25.5 7.9 %fetch_tiles.1 = bf16[512,128,128]{2,1,0:T(8,128)(2,1)} custom-call(s32[512]{0:T(512)} %all_to_all.12.asked_ref, bf16[128,128,128]{2,1,0:T(8,128)(2,1)} %tiles_ref.1), custom_call_target="tpu_custom_call" | custom-call | tf_op jit(solution)/shard_map/fetch_tiles/pallas_call | solution.py:111
  33.5 0.0 copy-start
  33.5 5.5 %all-to-all-start.1 = ((bf16[512,128,128]{2,1,0:T(8,128)(2,1)}), bf16[512,128,128]{2,1,0:T(8,128)(2,1)}, u32[]{:S(2)}, u32[]{:S(2)}) async-start(bf16[512,128,128]{2,1,0:T(8,128)(2,1)} %fetch_tiles.1), calls=%async_computation.1 | async-start | bytes 33554432 | tf_op jit(solution)/shard_map/all_to_all | solution.py:184
  39.0 0.0 copy-done
  39.0 0.6 multiply_add_fusion.slot_ref
  39.6 232.0 %all-to-all-done.1.reply_ref = bf16[512,128,128]{2,1,0:T(8,128)(2,1)} async-done(((bf16[512,128,128]{2,1,0:T(8,128)(2,1)}), bf16[512,128,128]{2,1,0:T(8,128)(2,1)}, u32[]{:S(2)}, u32[]{:S(2)}) %all-to-all-start.1) | async-done | bytes 16777248 | tf_op jit(solution)/shard_map/all_to_all | solution.py:184
  271.6 24.6 %region_work.1 = (bf16[512,128,128]{2,1,0:T(8,128)(2,1)}, f32[1,1024]{1,0:T(1,128)}) custom-call(s32[256]{0:T(256)} %multiply_add_fusion.slot_ref, bf16[1024,2048]{1,0:T(8,128)(2,1)} %bitcast.8, f32[1,1024]{1,0:T(1,128)} %weights_ref.1, bf16[512,128,128]{2,1,0:T(8,128)(2,1)} %all-to-all-done.1.reply_ref), custom_call_target="tpu_custom_call" | custom-call | tf_op jit(solution)/shard_map/region_work/pallas_call | solution.py:128
  296.1 208.3 %all_to_all.19.arrived_ref = bf16[512,128,128]{2,1,0:T(8,128)(2,1)} all-to-all(bf16[512,128,128]{2,1,0:T(8,128)(2,1)} %get-tuple-element.4), channel_id=1, replica_groups=mesh['row'=8,'col'=16] {'row','col'}, dimensions={0} | all-to-all | bytes 33554432 | tf_op jit(solution)/shard_map/all_to_all | solution.py:187
  504.4 13.5 %collect_tiles.1 = f32[128,128,128]{2,1,0:T(8,128)} custom-call(s32[512]{0:T(512)} %all_to_all.12.asked_ref, bf16[512,128,128]{2,1,0:T(8,128)(2,1)} %all_to_all.19.arrived_ref), custom_call_target="tpu_custom_call" | custom-call | tf_op jit(solution)/shard_map/collect_tiles/pallas_call | solution.py:149
  (2 shorter events, 0.0 us)
Async XLA Ops:
  33.5 5.5 %copy-start = (s32[1,256]{1,0:T(1,128)S(1)}, s32[1,256]{1,0:T(1,128)}, u32[]{:S(2)}) copy-start(s32[1,256]{1,0:T(1,128)} %param.7) | copy-start | bytes 3076
  33.5 238.1 %all-to-all-start.1 = ((bf16[512,128,128]{2,1,0:T(8,128)(2,1)}), bf16[512,128,128]{2,1,0:T(8,128)(2,1)}, u32[]{:S(2)}, u32[]{:S(2)}) async-start(bf16[512,128,128]{2,1,0:T(8,128)(2,1)} %fetch_tiles.1), calls=%async_computation.1 | async-start | bytes 33554432 | tf_op jit(solution)/shard_map/all_to_all | solution.py:184

commit v3 on v2

--- a/solution.py
+++ b/solution.py
@@ -181,7 +181,9 @@
     matches = (slot_of[None, :] == slot_ids[:, None]).astype(jnp.int32)
     send_local = jnp.sum(matches * (local_of + 1)[None, :], axis=1) - 1
     asked = exchange(send_local)
-    reply = exchange(fetch(asked, density_tiles))
+    fetched = fetch(asked, density_tiles)
+    fetched, slot_of, asked = lax.optimization_barrier((fetched, slot_of, asked))
+    reply = exchange(fetched)
     values = basis_values[0]
     outgoing, density = region(slot_of, values, grid_weights, reply)
     arrived = exchange(outgoing)

time: 519 us -> 459 us (0.88)
  waiting for transfers between devices: 232 us -> 8.43 us
  blocking collectives: 229 us -> 385 us
  starting transfers between devices: 5.52 us -> 11.5 us
    all_to_all x1, waiting for transfers between devices: 232 us -> 8.43 us  [per_device(): asked = exchange(send_local)]
    all_to_all x1, blocking collectives: 21.1 us -> 192 us  [per_device(): reply = exchange(fetched)]
    all_to_all x1, blocking collectives: 208 us -> 193 us  [per_device(): arrived = exchange(outgoing)]
    all_to_all x1, starting transfers between devices: 5.52 us -> 11.5 us  [per_device(): asked = exchange(send_local)]
where the time goes in v3:
time: 459 us; the launch traced here: 458 us
  blocking collectives  385 us (84%)
  Pallas kernels  46.1 us (10%)
  starting transfers between devices  11.5 us (3%)
  waiting for transfers between devices  8.43 us (2%)
    all_to_all x1, blocking collectives, per_device(): arrived = exchange(outgoing)  193 us
    all_to_all x1, blocking collectives, per_device(): reply = exchange(fetched)  192 us
    pallas_call x1, Pallas kernels, region(): pl.pallas_call(region_kernel, out_shape=(jax.ShapeDtypeStruct(reply.shape...  24.6 us
    pallas_call x1, Pallas kernels, collect(): pl.pallas_call(collect_kernel, out_shape=jax.ShapeDtypeStruct((stored,) +...  13.6 us
    all_to_all x1, starting transfers between devices, per_device(): asked = exchange(send_local)  11.5 us
  transfers between devices with their start and end apart: 1, of which 1 were waited for; matrix products, arithmetic and copies ran while one was open for 0% of the time, Pallas kernels for 0%

profile of v3, /device:TPU:1, one launch (start us, length us, event | category | flops | bytes accessed | tf_op | source)
XLA Modules:
  0.0 457.8 jit_solution(1080720887976275228)
XLA Ops:
  0.6 0.7 and_select_fusion.1
  1.3 0.7 and_select_fusion.2
  2.0 0.1 convert_reduce_fusion
  2.1 0.2 select_reduce_fusion
  2.3 0.7 sub.17
  3.0 11.5 %all-to-all-start = ((s32[128,4,1]{1,2,0:T(1,128)}), s32[128,4,1]{1,2,0:T(1,128)S(1)}, u32[]{:S(2)}, u32[]{:S(2)}) async-start(s32[128,4,1]{1,2,0:T(1,128)} %bitcast.5), calls=%async_computation | async-start | bytes 131072 | tf_op jit(solution)/shard_map/all_to_all | solution.py:183
  14.5 1.3 multiply_add_fusion.slot_ref
  15.8 8.4 %all-to-all-done = s32[128,4,1]{1,2,0:T(1,128)S(1)} async-done(((s32[128,4,1]{1,2,0:T(1,128)}), s32[128,4,1]{1,2,0:T(1,128)S(1)}, u32[]{:S(2)}, u32[]{:S(2)}) %all-to-all-start) | async-done | bytes 2080 | tf_op jit(solution)/shard_map/all_to_all | solution.py:183
  24.2 0.5 broadcast.99
  24.8 0.8 reduce.3
  25.6 0.7 all_to_all.12.asked_ref
  26.3 7.9 %fetch_tiles.1 = bf16[512,128,128]{2,1,0:T(8,128)(2,1)} custom-call(s32[512]{0:T(512)} %all_to_all.12.asked_ref, bf16[128,128,128]{2,1,0:T(8,128)(2,1)} %tiles_ref.1), custom_call_target="tpu_custom_call" | custom-call | tf_op jit(solution)/shard_map/fetch_tiles/pallas_call | solution.py:111
  34.2 192.0 %all_to_all.18.reply_ref = bf16[512,128,128]{2,1,0:T(8,128)(2,1)} all-to-all(bf16[512,128,128]{2,1,0:T(8,128)(2,1)} %fetch_tiles.1), channel_id=1, replica_groups=mesh['row'=8,'col'=16] {'row','col'}, dimensions={0} | all-to-all | bytes 33554432 | tf_op jit(solution)/shard_map/all_to_all | solution.py:186
  226.2 24.6 %region_work.1 = (bf16[512,128,128]{2,1,0:T(8,128)(2,1)}, f32[1,1024]{1,0:T(1,128)}) custom-call(s32[256]{0:T(256)} %multiply_add_fusion.slot_ref, bf16[1024,2048]{1,0:T(8,128)(2,1)} %bitcast.8, f32[1,1024]{1,0:T(1,128)} %weights_ref.1, bf16[512,128,128]{2,1,0:T(8,128)(2,1)} %all_to_all.18.reply_ref), custom_call_target="tpu_custom_call" | custom-call | tf_op jit(solution)/shard_map/region_work/pallas_call | solution.py:128
  250.8 193.3 %all_to_all.19.arrived_ref = bf16[512,128,128]{2,1,0:T(8,128)(2,1)} all-to-all(bf16[512,128,128]{2,1,0:T(8,128)(2,1)} %get-tuple-element.10), channel_id=1, replica_groups=mesh['row'=8,'col'=16] {'row','col'}, dimensions={0} | all-to-all | bytes 33554432 | tf_op jit(solution)/shard_map/all_to_all | solution.py:189
  444.1 13.6 %collect_tiles.1 = f32[128,128,128]{2,1,0:T(8,128)} custom-call(s32[512]{0:T(512)} %all_to_all.12.asked_ref, bf16[512,128,128]{2,1,0:T(8,128)(2,1)} %all_to_all.19.arrived_ref), custom_call_target="tpu_custom_call" | custom-call | tf_op jit(solution)/shard_map/collect_tiles/pallas_call | solution.py:149
  (2 shorter events, 0.0 us)
Async XLA Ops:
  3.0 21.2 %all-to-all-start = ((s32[128,4,1]{1,2,0:T(1,128)}), s32[128,4,1]{1,2,0:T(1,128)S(1)}, u32[]{:S(2)}, u32[]{:S(2)}) async-start(s32[128,4,1]{1,2,0:T(1,128)} %bitcast.5), calls=%async_computation | async-start | bytes 131072 | tf_op jit(solution)/shard_map/all_to_all | solution.py:183

commit v4 on v3

--- a/solution.py
+++ b/solution.py
@@ -10,6 +10,7 @@
 exchange_coeff = 0.9847450218426964
 AXES = ("row", "col")
 VMEM_BYTES = 56 * 1024 * 1024
+GROUP = 4
 
 
 def fetch_kernel(asked_ref, tiles_ref, out_ref, sem):
@@ -78,8 +79,9 @@
     pltpu.make_async_copy(partial, partial, store_sem).wait()
 
 
-def collect_kernel(asked_ref, arrived_ref, out_ref, held, sems):
+def collect_kernel(asked_ref, arrived_ref, out_ref, held, spare, seen, sems):
     slots = arrived_ref.shape[0]
+    stored = out_ref.shape[0]
     parts = sems.shape[0]
     size = slots // parts
 
@@ -90,20 +92,43 @@
 
     for j in range(parts):
         piece(j).start()
-    out_ref[...] = jnp.zeros_like(out_ref)
-
-    def add(slot, carry):
-        tile = asked_ref[slot]
-
-        @pl.when(tile >= 0)
-        def _():
-            out_ref[tile] = out_ref[tile] + held[slot].astype(jnp.float32)
-
+
+    def forget(tile, carry):
+        seen[tile] = 0
+        return carry
+
+    lax.fori_loop(0, stored + 1, forget, 0)
+
+    def add(group, carry):
+        base = group * GROUP
+        tiles = [asked_ref[base + k] for k in range(GROUP)]
+        tiles = [jnp.where(tile < 0, stored, tile) for tile in tiles]
+        kept = [seen[tile] > 0 for tile in tiles]
+        sums = []
+        for k in range(GROUP):
+            before = spare[tiles[k]]
+            sums.append(jnp.where(kept[k], before, 0.0) + held[base + k].astype(jnp.float32))
+        for k in range(GROUP):
+            spare[tiles[k]] = sums[k]
+            seen[tiles[k]] = 1
         return carry
 
     for j in range(parts):
         piece(j).wait()
-        lax.fori_loop(j * size, (j + 1) * size, add, 0)
+        lax.fori_loop(j * size // GROUP, (j + 1) * size // GROUP, add, 0)
+
+    def clear(tile, carry):
+        @pl.when(seen[tile] == 0)
+        def _():
+            spare[tile] = jnp.zeros(spare.shape[1:], jnp.float32)
+
+        return carry
+
+    lax.fori_loop(0, stored, clear, 0)
+    total = spare.at[pl.ds(0, stored)]
+    done = pltpu.make_async_copy(total, out_ref, sems.at[0])
+    done.start()
+    done.wait()
 
 
 def fetch(asked, tiles):
@@ -150,9 +175,11 @@
         collect_kernel,
         out_shape=jax.ShapeDtypeStruct((stored,) + arrived.shape[1:], jnp.float32),
         in_specs=[pl.BlockSpec(memory_space=pltpu.SMEM), pl.BlockSpec(memory_space=pl.ANY)],
-        out_specs=pl.BlockSpec(memory_space=pltpu.VMEM),
+        out_specs=pl.BlockSpec(memory_space=pl.ANY),
         scratch_shapes=[
             pltpu.VMEM(arrived.shape, jnp.bfloat16),
+            pltpu.VMEM((stored + 1,) + arrived.shape[1:], jnp.float32),
+            pltpu.SMEM((stored + 1,), jnp.int32),
             pltpu.SemaphoreType.DMA((8,)),
         ],
         compiler_params=pltpu.CompilerParams(vmem_limit_bytes=VMEM_BYTES),
@@ -180,11 +207,13 @@
     slot_ids = jnp.arange(slot_total, dtype=jnp.int32)
     matches = (slot_of[None, :] == slot_ids[:, None]).astype(jnp.int32)
     send_local = jnp.sum(matches * (local_of + 1)[None, :], axis=1) - 1
+    tiles = pltpu.with_memory_space_constraint(density_tiles, pltpu.VMEM)
+    send_local, tiles = lax.optimization_barrier((send_local, tiles))
     asked = exchange(send_local)
-    fetched = fetch(asked, density_tiles)
+    fetched = fetch(asked, tiles)
     fetched, slot_of, asked = lax.optimization_barrier((fetched, slot_of, asked))
     reply = exchange(fetched)
-    values = basis_values[0]
+    values = pltpu.with_memory_space_constraint(basis_values[0], pltpu.VMEM)
     outgoing, density = region(slot_of, values, grid_weights, reply)
     arrived = exchange(outgoing)
     return collect(asked, arrived, stored), density

time: 459 us -> 458 us (level)
  no operation moved by 1% of the time
where the time goes in v4:
time: 458 us
  blocking collectives  386 us (84%)
  Pallas kernels  43.6 us (10%)
  starting transfers between devices  11.5 us (3%)
  waiting for transfers between devices  8.43 us (2%)
    all_to_all x1, blocking collectives, per_device(): arrived = exchange(outgoing)  193 us
    all_to_all x1, blocking collectives, per_device(): reply = exchange(fetched)  192 us
    pallas_call x1, Pallas kernels, region(): pl.pallas_call(region_kernel, out_shape=(jax.ShapeDtypeStruct(reply.shape...  23.1 us
    pallas_call x1, Pallas kernels, collect(): pl.pallas_call(collect_kernel, out_shape=jax.ShapeDtypeStruct((stored,) +...  14.1 us
    all_to_all x1, starting transfers between devices, per_device(): asked = exchange(send_local)  11.5 us
  transfers between devices with their start and end apart: 1, of which 1 were waited for; matrix products, arithmetic and copies ran while one was open for 0% of the time, Pallas kernels for 0%

profile of v4, /device:TPU:1, one launch (start us, length us, event | category | flops | bytes accessed | tf_op | source)
XLA Modules:
  0.0 458.1 jit_solution(13437684477799555582)
XLA Ops:
  0.6 0.7 and_select_fusion.1
  1.3 0.7 and_select_fusion.2
  2.0 0.1 convert_reduce_fusion
  2.1 0.2 select_reduce_fusion
  2.3 0.7 all_to_all.13
  3.0 11.5 %all-to-all-start = ((s32[128,4,1]{1,2,0:T(1,128)}), s32[128,4,1]{1,2,0:T(1,128)S(1)}, u32[]{:S(2)}, u32[]{:S(2)}) async-start(s32[128,4,1]{1,2,0:T(1,128)} %bitcast.5), calls=%async_computation | async-start | bytes 131072 | tf_op jit(solution)/shard_map/all_to_all | solution.py:212
  14.5 1.3 multiply_add_fusion.slot_ref
  15.8 8.4 %all-to-all-done = s32[128,4,1]{1,2,0:T(1,128)S(1)} async-done(((s32[128,4,1]{1,2,0:T(1,128)}), s32[128,4,1]{1,2,0:T(1,128)S(1)}, u32[]{:S(2)}, u32[]{:S(2)}) %all-to-all-start) | async-done | bytes 2080 | tf_op jit(solution)/shard_map/all_to_all | solution.py:212
  24.2 0.5 broadcast.90
  24.8 0.8 reduce.3
  25.6 0.7 all_to_all.15.asked_ref
  26.3 0.0 copy-start
  26.3 2.2 copy-done
  28.5 6.4 %fetch_tiles.1 = bf16[512,128,128]{2,1,0:T(8,128)(2,1)} custom-call(s32[512]{0:T(512)} %all_to_all.15.asked_ref, bf16[128,128,128]{2,1,0:T(8,128)(2,1)S(1)} %copy-done), custom_call_target="tpu_custom_call" | custom-call | tf_op jit(solution)/shard_map/fetch_tiles/pallas_call | solution.py:136
  34.9 0.0 copy-start.1
  34.9 192.5 %all_to_all.21.reply_ref = bf16[512,128,128]{2,1,0:T(8,128)(2,1)} all-to-all(bf16[512,128,128]{2,1,0:T(8,128)(2,1)} %fetch_tiles.1), channel_id=1, replica_groups=mesh['row'=8,'col'=16] {'row','col'}, dimensions={0} | all-to-all | bytes 33554432 | tf_op jit(solution)/shard_map/all_to_all | solution.py:215
  227.4 0.0 copy-done.1
  227.4 23.1 %region_work.1 = (bf16[512,128,128]{2,1,0:T(8,128)(2,1)}, f32[1,1024]{1,0:T(1,128)}) custom-call(s32[256]{0:T(256)} %multiply_add_fusion.slot_ref, bf16[1024,2048]{1,0:T(8,128)(2,1)S(1)} %bitcast.8, f32[1,1024]{1,0:T(1,128)} %weights_ref.1, bf16[512,128,128]{2,1,0:T(8,128)(2,1)} %all_to_all.21.reply_ref), custom_call_target="tpu_custom_call" | custom-call | tf_op jit(solution)/shard_map/region_work/pallas_call | solution.py:153
  250.4 193.4 %all_to_all.22.arrived_ref = bf16[512,128,128]{2,1,0:T(8,128)(2,1)} all-to-all(bf16[512,128,128]{2,1,0:T(8,128)(2,1)} %get-tuple-element.14), channel_id=1, replica_groups=mesh['row'=8,'col'=16] {'row','col'}, dimensions={0} | all-to-all | bytes 33554432 | tf_op jit(solution)/shard_map/all_to_all | solution.py:218
  443.8 14.1 %collect_tiles.1 = f32[128,128,128]{2,1,0:T(8,128)} custom-call(s32[512]{0:T(512)} %all_to_all.15.asked_ref, bf16[512,128,128]{2,1,0:T(8,128)(2,1)} %all_to_all.22.arrived_ref), custom_call_target="tpu_custom_call" | custom-call | tf_op jit(solution)/shard_map/collect_tiles/pallas_call | solution.py:174
  (2 shorter events, 0.0 us)
Async XLA Ops:
  3.0 21.2 %all-to-all-start = ((s32[128,4,1]{1,2,0:T(1,128)}), s32[128,4,1]{1,2,0:T(1,128)S(1)}, u32[]{:S(2)}, u32[]{:S(2)}) async-start(s32[128,4,1]{1,2,0:T(1,128)} %bitcast.5), calls=%async_computation | async-start | bytes 131072 | tf_op jit(solution)/shard_map/all_to_all | solution.py:212
  26.3 2.2 copy-start
  34.9 192.5 %copy-start.1 = (bf16[1,1024,2048]{2,1,0:T(8,128)(2,1)S(1)}, bf16[1,1024,2048]{2,1,0:T(8,128)(2,1)}, u32[]{:S(2)}) copy-start(bf16[1,1024,2048]{2,1,0:T(8,128)(2,1)} %param.4) | copy-start | bytes 12582916

commit v5 on v3

--- a/solution.py
+++ b/solution.py
@@ -10,6 +10,8 @@
 exchange_coeff = 0.9847450218426964
 AXES = ("row", "col")
 VMEM_BYTES = 56 * 1024 * 1024
+GROUP = 4
+PARTS = 2
 
 
 def fetch_kernel(asked_ref, tiles_ref, out_ref, sem):
@@ -28,7 +30,7 @@
 
 def region_kernel(
     slot_ref, values_ref, weights_ref, reply_ref, out_ref, density_ref,
-    block, scaled, partial, load_sems, store_sem,
+    block, scaled, partial, store_sem,
 ):
     points, width_all = values_ref.shape
     width = reply_ref.shape[1]
@@ -36,22 +38,11 @@
     chunk = 4 * width
     chunks = width_all // chunk
 
-    def start_chunk(j):
+    total = jnp.zeros((points, width), jnp.float32)
+    for j in range(chunks):
         for q in range(4 * j, 4 * j + 4):
             for p in range(sig):
-                pltpu.make_async_copy(
-                    reply_ref.at[slot_ref[p * sig + q]], block.at[q, pl.ds(p * width, width)], load_sems.at[j]
-                ).start()
-
-    ahead = 2
-    for j in range(ahead):
-        start_chunk(j)
-    total = jnp.zeros((points, width), jnp.float32)
-    for j in range(chunks):
-        if j + ahead < chunks:
-            start_chunk(j + ahead)
-        pair = block.at[pl.ds(4 * j, 4)]
-        pltpu.make_async_copy(pair, pair, load_sems.at[j]).wait()
+                block[q, pl.ds(p * width, width)] = reply_ref[slot_ref[p * sig + q]]
         columns = jnp.concatenate([block[4 * j + k] for k in range(4)], axis=1)
         mixed = jnp.dot(values_ref[...], columns, preferred_element_type=jnp.float32)
         product = mixed * values_ref[:, pl.ds(j * chunk, chunk)].astype(jnp.float32)
@@ -78,32 +69,52 @@
     pltpu.make_async_copy(partial, partial, store_sem).wait()
 
 
-def collect_kernel(asked_ref, arrived_ref, out_ref, held, sems):
+def collect_kernel(asked_ref, arrived_ref, out_ref, held, seen, sems):
     slots = arrived_ref.shape[0]
+    stored, width = out_ref.shape[:2]
     parts = sems.shape[0]
-    size = slots // parts
-
-    def piece(j):
-        return pltpu.make_async_copy(
-            arrived_ref.at[pl.ds(j * size, size)], held.at[pl.ds(j * size, size)], sems.at[j]
-        )
-
-    for j in range(parts):
-        piece(j).start()
-    out_ref[...] = jnp.zeros_like(out_ref)
-
-    def add(slot, carry):
-        tile = asked_ref[slot]
-
-        @pl.when(tile >= 0)
+    height = width // parts
+
+    def forget(tile, carry):
+        seen[tile] = 0
+        return carry
+
+    lax.fori_loop(0, stored + 1, forget, 0, unroll=8)
+
+    def strip(part):
+        rows = pl.ds(part * height, height)
+        return pltpu.make_async_copy(held.at[pl.ds(0, stored), rows], out_ref.at[:, rows], sems.at[part])
+
+    def clear(tile, carry):
+        @pl.when(seen[tile] == 0)
         def _():
-            out_ref[tile] = out_ref[tile] + held[slot].astype(jnp.float32)
+            held[tile] = jnp.zeros(held.shape[1:], jnp.float32)
 
         return carry
 
-    for j in range(parts):
-        piece(j).wait()
-        lax.fori_loop(j * size, (j + 1) * size, add, 0)
+    for part in range(parts):
+        rows = pl.ds(part * height, height)
+
+        def add(group, carry):
+            base = group * GROUP
+            tiles = [asked_ref[base + k] for k in range(GROUP)]
+            tiles = [jnp.where(tile < 0, stored, tile) for tile in tiles]
+            kept = [seen[tile] > part for tile in tiles]
+            sums = []
+            for k in range(GROUP):
+                before = held[tiles[k], rows]
+                sums.append(jnp.where(kept[k], before, 0.0) + arrived_ref[base + k, rows].astype(jnp.float32))
+            for k in range(GROUP):
+                held[tiles[k], rows] = sums[k]
+                seen[tiles[k]] = part + 1
+            return carry
+
+        lax.fori_loop(0, slots // GROUP, add, 0)
+        if part == 0:
+            lax.fori_loop(0, stored, clear, 0)
+        strip(part).start()
+    for part in range(parts):
+        strip(part).wait()
 
 
 def fetch(asked, tiles):
@@ -122,7 +133,6 @@
 def region(slot_of, values, weights, reply):
     points, width_all = values.shape
     width = reply.shape[1]
-    chunks = width_all // (4 * width)
     vmem = pl.BlockSpec(memory_space=pltpu.VMEM)
     hbm = pl.BlockSpec(memory_space=pl.ANY)
     return pl.pallas_call(
@@ -131,16 +141,15 @@
             jax.ShapeDtypeStruct(reply.shape, jnp.bfloat16),
             jax.ShapeDtypeStruct((1, points), jnp.float32),
         ),
-        in_specs=[pl.BlockSpec(memory_space=pltpu.SMEM), vmem, vmem, hbm],
+        in_specs=[pl.BlockSpec(memory_space=pltpu.SMEM), vmem, vmem, vmem],
         out_specs=(hbm, vmem),
         scratch_shapes=[
             pltpu.VMEM((width_all // width, width_all, width), jnp.bfloat16),
             pltpu.VMEM((points, width_all), jnp.bfloat16),
             pltpu.VMEM((slot_of.shape[0], width, width), jnp.bfloat16),
-            pltpu.SemaphoreType.DMA((chunks,)),
             pltpu.SemaphoreType.DMA,
         ],
-        compiler_params=pltpu.CompilerParams(vmem_limit_bytes=VMEM_BYTES),
+        compiler_params=pltpu.CompilerParams(vmem_limit_bytes=34 * 1024 * 1024),
         name="region_work",
     )(slot_of, values, weights, reply)
 
@@ -149,13 +158,14 @@
     return pl.pallas_call(
         collect_kernel,
         out_shape=jax.ShapeDtypeStruct((stored,) + arrived.shape[1:], jnp.float32),
-        in_specs=[pl.BlockSpec(memory_space=pltpu.SMEM), pl.BlockSpec(memory_space=pl.ANY)],
-        out_specs=pl.BlockSpec(memory_space=pltpu.VMEM),
+        in_specs=[pl.BlockSpec(memory_space=pltpu.SMEM), pl.BlockSpec(memory_space=pltpu.VMEM)],
+        out_specs=pl.BlockSpec(memory_space=pl.ANY),
         scratch_shapes=[
-            pltpu.VMEM(arrived.shape, jnp.bfloat16),
-            pltpu.SemaphoreType.DMA((8,)),
+            pltpu.VMEM((stored + 1,) + arrived.shape[1:], jnp.float32),
+            pltpu.SMEM((stored + 1,), jnp.int32),
+            pltpu.SemaphoreType.DMA((PARTS,)),
         ],
-        compiler_params=pltpu.CompilerParams(vmem_limit_bytes=VMEM_BYTES),
+        compiler_params=pltpu.CompilerParams(vmem_limit_bytes=20 * 1024 * 1024),
         name="collect_tiles",
     )(asked, arrived)
 
@@ -183,10 +193,10 @@
     asked = exchange(send_local)
     fetched = fetch(asked, density_tiles)
     fetched, slot_of, asked = lax.optimization_barrier((fetched, slot_of, asked))
-    reply = exchange(fetched)
-    values = basis_values[0]
+    reply = pltpu.with_memory_space_constraint(exchange(fetched), pltpu.VMEM)
+    values = pltpu.with_memory_space_constraint(basis_values[0], pltpu.VMEM)
     outgoing, density = region(slot_of, values, grid_weights, reply)
-    arrived = exchange(outgoing)
+    arrived = pltpu.with_memory_space_constraint(exchange(outgoing), pltpu.VMEM)
     return collect(asked, arrived, stored), density
 
 

time: 459 us -> 454 us (0.989)
  no operation moved by 1% of the time
where the time goes in v5:
time: 454 us; the launch traced here: 453 us
  blocking collectives  385 us (85%)
  Pallas kernels  41.9 us (9%)
  starting transfers between devices  11.5 us (3%)
  waiting for transfers between devices  8.44 us (2%)
    all_to_all x1, blocking collectives, per_device(): arrived = pltpu.with_memory_space_constraint(exchange(outgoing), pltpu.VMEM)  193 us
    all_to_all x1, blocking collectives, per_device(): reply = pltpu.with_memory_space_constraint(exchange(fetched), pltpu.VMEM)  192 us
    pallas_call x1, Pallas kernels, region(): pl.pallas_call(region_kernel, out_shape=(jax.ShapeDtypeStruct(reply.shape...  21.7 us
    pallas_call x1, Pallas kernels, collect(): pl.pallas_call(collect_kernel, out_shape=jax.ShapeDtypeStruct((stored,) +...  12.2 us
    all_to_all x1, starting transfers between devices, per_device(): asked = exchange(send_local)  11.5 us
  transfers between devices with their start and end apart: 1, of which 1 were waited for; matrix products, arithmetic and copies ran while one was open for 0% of the time, Pallas kernels for 0%

profile of v5, /device:TPU:1, one launch (start us, length us, event | category | flops | bytes accessed | tf_op | source)
XLA Modules:
  0.0 453.3 jit_solution(1812339363253148651)
XLA Ops:
  0.6 0.7 and_select_fusion.1
  1.3 0.7 and_select_fusion.2
  2.0 0.1 convert_reduce_fusion
  2.1 0.2 select_reduce_fusion
  2.3 0.7 sub.17
  3.0 11.5 %all-to-all-start = ((s32[128,4,1]{1,2,0:T(1,128)}), s32[128,4,1]{1,2,0:T(1,128)S(1)}, u32[]{:S(2)}, u32[]{:S(2)}) async-start(s32[128,4,1]{1,2,0:T(1,128)} %bitcast.5), calls=%async_computation | async-start | bytes 131072 | tf_op jit(solution)/shard_map/all_to_all | solution.py:193
  14.5 1.3 multiply_add_fusion.slot_ref
  15.8 8.4 %all-to-all-done = s32[128,4,1]{1,2,0:T(1,128)S(1)} async-done(((s32[128,4,1]{1,2,0:T(1,128)}), s32[128,4,1]{1,2,0:T(1,128)S(1)}, u32[]{:S(2)}, u32[]{:S(2)}) %all-to-all-start) | async-done | bytes 2080 | tf_op jit(solution)/shard_map/all_to_all | solution.py:193
  24.2 0.5 broadcast.99
  24.8 0.8 reduce.3
  25.6 0.7 all_to_all.12.asked_ref
  26.3 7.9 %fetch_tiles.1 = bf16[512,128,128]{2,1,0:T(8,128)(2,1)} custom-call(s32[512]{0:T(512)} %all_to_all.12.asked_ref, bf16[128,128,128]{2,1,0:T(8,128)(2,1)} %tiles_ref.1), custom_call_target="tpu_custom_call" | custom-call | tf_op jit(solution)/shard_map/fetch_tiles/pallas_call | solution.py:122
  34.2 0.0 copy-start
  34.2 191.7 %all_to_all.18.reply_ref = bf16[512,128,128]{2,1,0:T(8,128)(2,1)S(1)} all-to-all(bf16[512,128,128]{2,1,0:T(8,128)(2,1)} %fetch_tiles.1), channel_id=1, replica_groups=mesh['row'=8,'col'=16] {'row','col'}, dimensions={0} | all-to-all | bytes 33554432 | tf_op jit(solution)/shard_map/all_to_all | solution.py:196
  225.9 0.0 copy-done
  225.9 21.7 %region_work.1 = (bf16[512,128,128]{2,1,0:T(8,128)(2,1)}, f32[1,1024]{1,0:T(1,128)}) custom-call(s32[256]{0:T(256)} %multiply_add_fusion.slot_ref, bf16[1024,2048]{1,0:T(8,128)(2,1)S(1)} %bitcast.8, f32[1,1024]{1,0:T(1,128)} %weights_ref.1, bf16[512,128,128]{2,1,0:T(8,128)(2,1)S(1)} %all_to_all.18.reply_ref), custom_call_target="tpu_custom_call" | custom-call | tf_op jit(solution)/shard_map/region_work/pallas_call | solution.py:138
  247.7 0.0 copy-start.1
  247.7 193.3 %all_to_all.19.arrived_ref = bf16[512,128,128]{2,1,0:T(8,128)(2,1)S(1)} all-to-all(bf16[512,128,128]{2,1,0:T(8,128)(2,1)} %get-tuple-element.10), channel_id=1, replica_groups=mesh['row'=8,'col'=16] {'row','col'}, dimensions={0} | all-to-all | bytes 33554432 | tf_op jit(solution)/shard_map/all_to_all | solution.py:199
  440.9 0.0 copy-done.1
  440.9 12.2 %collect_tiles.1 = f32[128,128,128]{2,1,0:T(8,128)} custom-call(s32[512]{0:T(512)S(1)} %copy-done.1, bf16[512,128,128]{2,1,0:T(8,128)(2,1)S(1)} %all_to_all.19.arrived_ref), custom_call_target="tpu_custom_call" | custom-call | tf_op jit(solution)/shard_map/collect_tiles/pallas_call | solution.py:158
  (2 shorter events, 0.0 us)
Async XLA Ops:
  3.0 21.2 %all-to-all-start = ((s32[128,4,1]{1,2,0:T(1,128)}), s32[128,4,1]{1,2,0:T(1,128)S(1)}, u32[]{:S(2)}, u32[]{:S(2)}) async-start(s32[128,4,1]{1,2,0:T(1,128)} %bitcast.5), calls=%async_computation | async-start | bytes 131072 | tf_op jit(solution)/shard_map/all_to_all | solution.py:193
  34.2 191.7 %copy-start = (bf16[1,1024,2048]{2,1,0:T(8,128)(2,1)S(1)}, bf16[1,1024,2048]{2,1,0:T(8,128)(2,1)}, u32[]{:S(2)}) copy-start(bf16[1,1024,2048]{2,1,0:T(8,128)(2,1)} %param.4) | copy-start | bytes 12582916
  247.7 193.3 %copy-start.1 = (s32[512]{0:T(512)S(1)}, s32[512]{0:T(512)}, u32[]{:S(2)}) copy-start(s32[512]{0:T(512)} %all_to_all.12.asked_ref) | copy-start | bytes 6148

commit v6 on v5

--- a/solution.py
+++ b/solution.py
@@ -20,7 +20,7 @@
     def start(step, carry):
         for lane in range(8):
             slot = step * 8 + lane
-            tile = jnp.maximum(asked_ref[slot], 0)
+            tile = jnp.maximum(asked_ref[step * (8 // GROUP) + lane // GROUP, lane % GROUP], 0)
             pltpu.make_async_copy(tiles_ref.at[tile], out_ref.at[slot], sem).start()
         return carry
 
@@ -97,7 +97,7 @@
 
         def add(group, carry):
             base = group * GROUP
-            tiles = [asked_ref[base + k] for k in range(GROUP)]
+            tiles = [asked_ref[group, k] for k in range(GROUP)]
             tiles = [jnp.where(tile < 0, stored, tile) for tile in tiles]
             kept = [seen[tile] > part for tile in tiles]
             sums = []
@@ -118,7 +118,7 @@
 
 
 def fetch(asked, tiles):
-    slots = asked.shape[0]
+    slots = asked.shape[0] * GROUP
     return pl.pallas_call(
         fetch_kernel,
         out_shape=jax.ShapeDtypeStruct((slots,) + tiles.shape[1:], tiles.dtype),
@@ -175,7 +175,6 @@
     stored = density_tiles.shape[0]
     pairs = tile_index.shape[1]
     capacity = 2 * pairs // devices
-    slot_total = devices * capacity
     exchange = functools.partial(
         lax.all_to_all, axis_name=AXES, split_axis=0, concat_axis=0, tiled=True
     )
@@ -187,10 +186,12 @@
     same_owner = owner_of[:, None] == owner_of[None, :]
     position = jnp.sum((same_owner & earlier).astype(jnp.int32), axis=0)
     slot_of = owner_of * capacity + position
-    slot_ids = jnp.arange(slot_total, dtype=jnp.int32)
-    matches = (slot_of[None, :] == slot_ids[:, None]).astype(jnp.int32)
-    send_local = jnp.sum(matches * (local_of + 1)[None, :], axis=1) - 1
-    asked = exchange(send_local)
+    device_ids = jnp.arange(devices, dtype=jnp.int32)
+    lanes = jnp.arange(stored, dtype=jnp.int32)
+    to_owner = (owner_of[None, :] == device_ids[:, None]).astype(jnp.bfloat16)
+    named = jnp.where(position[:, None] == lanes[None, :], (local_of + 1)[:, None], 0)
+    send_local = jnp.dot(to_owner, named.astype(jnp.bfloat16), preferred_element_type=jnp.float32)
+    asked = exchange(send_local.astype(jnp.int32) - 1)
     fetched = fetch(asked, density_tiles)
     fetched, slot_of, asked = lax.optimization_barrier((fetched, slot_of, asked))
     reply = pltpu.with_memory_space_constraint(exchange(fetched), pltpu.VMEM)

time: 454 us -> 453 us (level)
  no operation moved by 1% of the time
where the time goes in v6:
time: 453 us
  blocking collectives  385 us (85%)
  Pallas kernels  42.9 us (9%)
  starting transfers between devices  11.5 us (3%)
  waiting for transfers between devices  9.16 us (2%)
    all_to_all x1, blocking collectives, per_device(): arrived = pltpu.with_memory_space_constraint(exchange(outgoing), pltpu.VMEM)  193 us
    all_to_all x1, blocking collectives, per_device(): reply = pltpu.with_memory_space_constraint(exchange(fetched), pltpu.VMEM)  192 us
    pallas_call x1, Pallas kernels, region(): pl.pallas_call(region_kernel, out_shape=(jax.ShapeDtypeStruct(reply.shape...  21.8 us
    pallas_call x1, Pallas kernels, collect(): pl.pallas_call(collect_kernel, out_shape=jax.ShapeDtypeStruct((stored,) +...  13.3 us
    all_to_all x1, starting transfers between devices, per_device(): asked = exchange(send_local.astype(jnp.int32) - 1)  11.5 us
    all_to_all x1, waiting for transfers between devices, per_device(): asked = exchange(send_local.astype(jnp.int32) - 1)  9.16 us
  transfers between devices with their start and end apart: 1, of which 1 were waited for; matrix products, arithmetic and copies ran while one was open for 0% of the time, Pallas kernels for 0%

profile of v6, /device:TPU:1, one launch (start us, length us, event | category | flops | bytes accessed | tf_op | source)
XLA Modules:
  0.0 453.0 jit_solution(2006379584263716545)
XLA Ops:
  0.6 0.7 and_select_fusion
  1.3 0.7 and_select_fusion.2
  2.0 0.1 convert_reduce_fusion
  2.1 0.9 fusion
  3.0 11.5 %all-to-all-start = ((s32[128,1,128]{2,1,0:T(1,128)}), s32[128,1,128]{2,1,0:T(1,128)S(1)}, u32[]{:S(2)}, u32[]{:S(2)}) async-start(s32[128,1,128]{2,1,0:T(1,128)} %bitcast.3), calls=%async_computation | async-start | bytes 131072 | tf_op jit(solution)/shard_map/all_to_all | solution.py:194
  14.5 0.5 multiply_add_fusion.slot_ref
  15.1 9.2 %all-to-all-done = s32[128,1,128]{2,1,0:T(1,128)S(1)} async-done(((s32[128,1,128]{2,1,0:T(1,128)}), s32[128,1,128]{2,1,0:T(1,128)S(1)}, u32[]{:S(2)}, u32[]{:S(2)}) %all-to-all-start) | async-done | bytes 65568 | tf_op jit(solution)/shard_map/all_to_all | solution.py:194
  24.2 0.0 copy-start.1
  24.2 0.6 copy-done.1
  24.9 7.9 %fetch_tiles.1 = bf16[512,128,128]{2,1,0:T(8,128)(2,1)} custom-call(s32[128,128]{1,0:T(8,128)} %bitcast.8, bf16[128,128,128]{2,1,0:T(8,128)(2,1)} %tiles_ref.1), custom_call_target="tpu_custom_call" | custom-call | tf_op jit(solution)/shard_map/fetch_tiles/pallas_call | solution.py:122
  32.8 0.0 copy-start
  32.8 191.7 %all_to_all.21.reply_ref = bf16[512,128,128]{2,1,0:T(8,128)(2,1)S(1)} all-to-all(bf16[512,128,128]{2,1,0:T(8,128)(2,1)} %fetch_tiles.1), channel_id=1, replica_groups=mesh['row'=8,'col'=16] {'row','col'}, dimensions={0} | all-to-all | bytes 33554432 | tf_op jit(solution)/shard_map/all_to_all | solution.py:197
  224.6 0.0 copy-done
  224.6 21.8 %region_work.1 = (bf16[512,128,128]{2,1,0:T(8,128)(2,1)}, f32[1,1024]{1,0:T(1,128)}) custom-call(s32[256]{0:T(256)} %multiply_add_fusion.slot_ref, bf16[1024,2048]{1,0:T(8,128)(2,1)S(1)} %bitcast.7, f32[1,1024]{1,0:T(1,128)} %weights_ref.1, bf16[512,128,128]{2,1,0:T(8,128)(2,1)S(1)} %all_to_all.21.reply_ref), custom_call_target="tpu_custom_call" | custom-call | tf_op jit(solution)/shard_map/region_work/pallas_call | solution.py:138
  246.3 0.0 copy-start.2
  246.3 193.2 %all_to_all.22.arrived_ref = bf16[512,128,128]{2,1,0:T(8,128)(2,1)S(1)} all-to-all(bf16[512,128,128]{2,1,0:T(8,128)(2,1)} %get-tuple-element.10), channel_id=1, replica_groups=mesh['row'=8,'col'=16] {'row','col'}, dimensions={0} | all-to-all | bytes 33554432 | tf_op jit(solution)/shard_map/all_to_all | solution.py:200
  439.6 0.0 copy-done.2
  439.6 13.3 %collect_tiles.1 = f32[128,128,128]{2,1,0:T(8,128)} custom-call(s32[128,128]{1,0:T(8,128)S(1)} %bitcast.9, bf16[512,128,128]{2,1,0:T(8,128)(2,1)S(1)} %all_to_all.22.arrived_ref), custom_call_target="tpu_custom_call" | custom-call | tf_op jit(solution)/shard_map/collect_tiles/pallas_call | solution.py:158
Async XLA Ops:
  3.0 21.2 %all-to-all-start = ((s32[128,1,128]{2,1,0:T(1,128)}), s32[128,1,128]{2,1,0:T(1,128)S(1)}, u32[]{:S(2)}, u32[]{:S(2)}) async-start(s32[128,1,128]{2,1,0:T(1,128)} %bitcast.3), calls=%async_computation | async-start | bytes 131072 | tf_op jit(solution)/shard_map/all_to_all | solution.py:194
  24.2 0.6 copy-start.1
  32.8 191.7 %copy-start = (bf16[1,1024,2048]{2,1,0:T(8,128)(2,1)S(1)}, bf16[1,1024,2048]{2,1,0:T(8,128)(2,1)}, u32[]{:S(2)}) copy-start(bf16[1,1024,2048]{2,1,0:T(8,128)(2,1)} %param.4) | copy-start | bytes 12582916
  246.3 193.2 %copy-start.2 = (s32[128,1,128]{2,1,0:T(1,128)S(1)}, s32[128,1,128]{2,1,0:T(1,128)}, u32[]{:S(2)}) copy-start(s32[128,1,128]{2,1,0:T(1,128)} %copy-done.1) | copy-start | bytes 196612

commit v7 on v6

--- a/solution.py
+++ b/solution.py
@@ -14,13 +14,15 @@
 PARTS = 2
 
 
-def fetch_kernel(asked_ref, tiles_ref, out_ref, sem):
+def fetch_kernel(asked_ref, tiles_ref, out_ref, flat_ref, sem):
     slots = out_ref.shape[0]
 
     def start(step, carry):
         for lane in range(8):
             slot = step * 8 + lane
-            tile = jnp.maximum(asked_ref[step * (8 // GROUP) + lane // GROUP, lane % GROUP], 0)
+            named = asked_ref[step * (8 // GROUP) + lane // GROUP, lane % GROUP]
+            flat_ref[slot] = named
+            tile = jnp.maximum(named, 0)
             pltpu.make_async_copy(tiles_ref.at[tile], out_ref.at[slot], sem).start()
         return carry
 
@@ -97,7 +99,7 @@
 
         def add(group, carry):
             base = group * GROUP
-            tiles = [asked_ref[group, k] for k in range(GROUP)]
+            tiles = [asked_ref[base + k] for k in range(GROUP)]
             tiles = [jnp.where(tile < 0, stored, tile) for tile in tiles]
             kept = [seen[tile] > part for tile in tiles]
             sums = []
@@ -121,9 +123,12 @@
     slots = asked.shape[0] * GROUP
     return pl.pallas_call(
         fetch_kernel,
-        out_shape=jax.ShapeDtypeStruct((slots,) + tiles.shape[1:], tiles.dtype),
+        out_shape=(
+            jax.ShapeDtypeStruct((slots,) + tiles.shape[1:], tiles.dtype),
+            jax.ShapeDtypeStruct((slots,), jnp.int32),
+        ),
         in_specs=[pl.BlockSpec(memory_space=pltpu.SMEM), pl.BlockSpec(memory_space=pltpu.VMEM)],
-        out_specs=pl.BlockSpec(memory_space=pl.ANY),
+        out_specs=(pl.BlockSpec(memory_space=pl.ANY), pl.BlockSpec(memory_space=pltpu.SMEM)),
         scratch_shapes=[pltpu.SemaphoreType.DMA],
         compiler_params=pltpu.CompilerParams(vmem_limit_bytes=VMEM_BYTES),
         name="fetch_tiles",
@@ -192,7 +197,7 @@
     named = jnp.where(position[:, None] == lanes[None, :], (local_of + 1)[:, None], 0)
     send_local = jnp.dot(to_owner, named.astype(jnp.bfloat16), preferred_element_type=jnp.float32)
     asked = exchange(send_local.astype(jnp.int32) - 1)
-    fetched = fetch(asked, density_tiles)
+    fetched, asked = fetch(asked, density_tiles)
     fetched, slot_of, asked = lax.optimization_barrier((fetched, slot_of, asked))
     reply = pltpu.with_memory_space_constraint(exchange(fetched), pltpu.VMEM)
     values = pltpu.with_memory_space_constraint(basis_values[0], pltpu.VMEM)

time: 453 us -> 453 us (level)
  no operation moved by 1% of the time
where the time goes in v7:
time: 453 us; the launch traced here: 452 us
  blocking collectives  385 us (85%)
  Pallas kernels  42.5 us (9%)
  starting transfers between devices  11.5 us (3%)
  waiting for transfers between devices  9.13 us (2%)
    all_to_all x1, blocking collectives, per_device(): arrived = pltpu.with_memory_space_constraint(exchange(outgoing), pltpu.VMEM)  193 us
    all_to_all x1, blocking collectives, per_device(): reply = pltpu.with_memory_space_constraint(exchange(fetched), pltpu.VMEM)  192 us
    pallas_call x1, Pallas kernels, region(): pl.pallas_call(region_kernel, out_shape=(jax.ShapeDtypeStruct(reply.shape...  21.7 us
    pallas_call x1, Pallas kernels, collect(): pl.pallas_call(collect_kernel, out_shape=jax.ShapeDtypeStruct((stored,) +...  12.2 us
    all_to_all x1, starting transfers between devices, per_device(): asked = exchange(send_local.astype(jnp.int32) - 1)  11.5 us
    all_to_all x1, waiting for transfers between devices, per_device(): asked = exchange(send_local.astype(jnp.int32) - 1)  9.13 us
  transfers between devices with their start and end apart: 1, of which 1 were waited for; matrix products, arithmetic and copies ran while one was open for 0% of the time, Pallas kernels for 0%

profile of v7, /device:TPU:1, one launch (start us, length us, event | category | flops | bytes accessed | tf_op | source)
XLA Modules:
  0.0 452.5 jit_solution(6121050230396346531)
XLA Ops:
  0.6 0.7 and_select_fusion
  1.3 0.7 and_select_fusion.2
  2.0 0.1 convert_reduce_fusion
  2.1 0.9 fusion
  3.0 11.5 %all-to-all-start = ((s32[128,1,128]{2,1,0:T(1,128)}), s32[128,1,128]{2,1,0:T(1,128)S(1)}, u32[]{:S(2)}, u32[]{:S(2)}) async-start(s32[128,1,128]{2,1,0:T(1,128)} %bitcast.3), calls=%async_computation | async-start | bytes 131072 | tf_op jit(solution)/shard_map/all_to_all | solution.py:199
  14.5 0.6 multiply_add_fusion.slot_ref
  15.1 9.1 %all-to-all-done = s32[128,1,128]{2,1,0:T(1,128)S(1)} async-done(((s32[128,1,128]{2,1,0:T(1,128)}), s32[128,1,128]{2,1,0:T(1,128)S(1)}, u32[]{:S(2)}, u32[]{:S(2)}) %all-to-all-start) | async-done | bytes 65568 | tf_op jit(solution)/shard_map/all_to_all | solution.py:199
  24.2 0.0 copy-start.2
  24.2 0.6 copy-done.2
  24.9 8.5 %fetch_tiles.1 = (bf16[512,128,128]{2,1,0:T(8,128)(2,1)}, s32[512]{0:T(512)}) custom-call(s32[128,128]{1,0:T(8,128)} %bitcast.8, bf16[128,128,128]{2,1,0:T(8,128)(2,1)} %tiles_ref.1), custom_call_target="tpu_custom_call" | custom-call | tf_op jit(solution)/shard_map/fetch_tiles/pallas_call | solution.py:124
  33.4 0.0 copy-start
  33.4 191.7 %all_to_all.21.reply_ref = bf16[512,128,128]{2,1,0:T(8,128)(2,1)S(1)} all-to-all(bf16[512,128,128]{2,1,0:T(8,128)(2,1)} %get-tuple-element.13), channel_id=1, replica_groups=mesh['row'=8,'col'=16] {'row','col'}, dimensions={0} | all-to-all | bytes 33554432 | tf_op jit(solution)/shard_map/all_to_all | solution.py:202
  225.1 0.0 copy-done
  225.1 21.7 %region_work.1 = (bf16[512,128,128]{2,1,0:T(8,128)(2,1)}, f32[1,1024]{1,0:T(1,128)}) custom-call(s32[256]{0:T(256)} %multiply_add_fusion.slot_ref, bf16[1024,2048]{1,0:T(8,128)(2,1)S(1)} %bitcast.7, f32[1,1024]{1,0:T(1,128)} %weights_ref.1, bf16[512,128,128]{2,1,0:T(8,128)(2,1)S(1)} %all_to_all.21.reply_ref), custom_call_target="tpu_custom_call" | custom-call | tf_op jit(solution)/shard_map/region_work/pallas_call | solution.py:143
  246.9 0.0 copy-start.1
  246.9 193.2 %all_to_all.22.arrived_ref = bf16[512,128,128]{2,1,0:T(8,128)(2,1)S(1)} all-to-all(bf16[512,128,128]{2,1,0:T(8,128)(2,1)} %get-tuple-element.14), channel_id=1, replica_groups=mesh['row'=8,'col'=16] {'row','col'}, dimensions={0} | all-to-all | bytes 33554432 | tf_op jit(solution)/shard_map/all_to_all | solution.py:205
  440.1 0.0 copy-done.1
  440.1 12.2 %collect_tiles.1 = f32[128,128,128]{2,1,0:T(8,128)} custom-call(s32[512]{0:T(512)S(1)} %copy-done.1, bf16[512,128,128]{2,1,0:T(8,128)(2,1)S(1)} %all_to_all.22.arrived_ref), custom_call_target="tpu_custom_call" | custom-call | tf_op jit(solution)/shard_map/collect_tiles/pallas_call | solution.py:163
Async XLA Ops:
  3.0 21.2 %all-to-all-start = ((s32[128,1,128]{2,1,0:T(1,128)}), s32[128,1,128]{2,1,0:T(1,128)S(1)}, u32[]{:S(2)}, u32[]{:S(2)}) async-start(s32[128,1,128]{2,1,0:T(1,128)} %bitcast.3), calls=%async_computation | async-start | bytes 131072 | tf_op jit(solution)/shard_map/all_to_all | solution.py:199
  24.2 0.6 copy-start.2
  33.4 191.7 %copy-start = (bf16[1,1024,2048]{2,1,0:T(8,128)(2,1)S(1)}, bf16[1,1024,2048]{2,1,0:T(8,128)(2,1)}, u32[]{:S(2)}) copy-start(bf16[1,1024,2048]{2,1,0:T(8,128)(2,1)} %param.4) | copy-start | bytes 12582916
  246.9 193.2 %copy-start.1 = (s32[512]{0:T(512)S(1)}, s32[512]{0:T(512)}, u32[]{:S(2)}) copy-start(s32[512]{0:T(512)} %get-tuple-element.11.asked_ref) | copy-start | bytes 6148

commit v8 on v7

--- a/solution.py
+++ b/solution.py
@@ -18,15 +18,15 @@
     slots = out_ref.shape[0]
 
     def start(step, carry):
-        for lane in range(8):
-            slot = step * 8 + lane
-            named = asked_ref[step * (8 // GROUP) + lane // GROUP, lane % GROUP]
+        for lane in range(16):
+            slot = step * 16 + lane
+            named = asked_ref[step * (16 // GROUP) + lane // GROUP, lane % GROUP]
             flat_ref[slot] = named
             tile = jnp.maximum(named, 0)
             pltpu.make_async_copy(tiles_ref.at[tile], out_ref.at[slot], sem).start()
         return carry
 
-    lax.fori_loop(0, slots // 8, start, 0)
+    lax.fori_loop(0, slots // 16, start, 0)
     pltpu.make_async_copy(out_ref, out_ref, sem).wait()
 
 

time: 453 us -> 453 us (level)
  no operation moved by 1% of the time
where the time goes in v8:
time: 453 us
  blocking collectives  385 us (85%)
  Pallas kernels  42.4 us (9%)
  starting transfers between devices  11.5 us (3%)
  waiting for transfers between devices  9.13 us (2%)
    all_to_all x1, blocking collectives, per_device(): arrived = pltpu.with_memory_space_constraint(exchange(outgoing), pltpu.VMEM)  193 us
    all_to_all x1, blocking collectives, per_device(): reply = pltpu.with_memory_space_constraint(exchange(fetched), pltpu.VMEM)  192 us
    pallas_call x1, Pallas kernels, region(): pl.pallas_call(region_kernel, out_shape=(jax.ShapeDtypeStruct(reply.shape...  21.7 us
    pallas_call x1, Pallas kernels, collect(): pl.pallas_call(collect_kernel, out_shape=jax.ShapeDtypeStruct((stored,) +...  12.2 us
    all_to_all x1, starting transfers between devices, per_device(): asked = exchange(send_local.astype(jnp.int32) - 1)  11.5 us
    all_to_all x1, waiting for transfers between devices, per_device(): asked = exchange(send_local.astype(jnp.int32) - 1)  9.13 us
  transfers between devices with their start and end apart: 1, of which 1 were waited for; matrix products, arithmetic and copies ran while one was open for 0% of the time, Pallas kernels for 0%

profile of v8, /device:TPU:1, one launch (start us, length us, event | category | flops | bytes accessed | tf_op | source)
XLA Modules:
  0.0 452.5 jit_solution(13429346687013345025)
XLA Ops:
  0.6 0.7 and_select_fusion
  1.3 0.7 and_select_fusion.2
  2.0 0.1 convert_reduce_fusion
  2.1 0.9 fusion
  3.0 11.5 %all-to-all-start = ((s32[128,1,128]{2,1,0:T(1,128)}), s32[128,1,128]{2,1,0:T(1,128)S(1)}, u32[]{:S(2)}, u32[]{:S(2)}) async-start(s32[128,1,128]{2,1,0:T(1,128)} %bitcast.3), calls=%async_computation | async-start | bytes 131072 | tf_op jit(solution)/shard_map/all_to_all | solution.py:199
  14.5 0.6 multiply_add_fusion.slot_ref
  15.1 9.1 %all-to-all-done = s32[128,1,128]{2,1,0:T(1,128)S(1)} async-done(((s32[128,1,128]{2,1,0:T(1,128)}), s32[128,1,128]{2,1,0:T(1,128)S(1)}, u32[]{:S(2)}, u32[]{:S(2)}) %all-to-all-start) | async-done | bytes 65568 | tf_op jit(solution)/shard_map/all_to_all | solution.py:199
  24.2 0.0 copy-start.2
  24.2 0.6 copy-done.2
  24.9 8.5 %fetch_tiles.1 = (bf16[512,128,128]{2,1,0:T(8,128)(2,1)}, s32[512]{0:T(512)}) custom-call(s32[128,128]{1,0:T(8,128)} %bitcast.8, bf16[128,128,128]{2,1,0:T(8,128)(2,1)} %tiles_ref.1), custom_call_target="tpu_custom_call" | custom-call | tf_op jit(solution)/shard_map/fetch_tiles/pallas_call | solution.py:124
  33.4 0.0 copy-start
  33.4 191.7 %all_to_all.21.reply_ref = bf16[512,128,128]{2,1,0:T(8,128)(2,1)S(1)} all-to-all(bf16[512,128,128]{2,1,0:T(8,128)(2,1)} %get-tuple-element.13), channel_id=1, replica_groups=mesh['row'=8,'col'=16] {'row','col'}, dimensions={0} | all-to-all | bytes 33554432 | tf_op jit(solution)/shard_map/all_to_all | solution.py:202
  225.1 0.0 copy-done
  225.1 21.7 %region_work.1 = (bf16[512,128,128]{2,1,0:T(8,128)(2,1)}, f32[1,1024]{1,0:T(1,128)}) custom-call(s32[256]{0:T(256)} %multiply_add_fusion.slot_ref, bf16[1024,2048]{1,0:T(8,128)(2,1)S(1)} %bitcast.7, f32[1,1024]{1,0:T(1,128)} %weights_ref.1, bf16[512,128,128]{2,1,0:T(8,128)(2,1)S(1)} %all_to_all.21.reply_ref), custom_call_target="tpu_custom_call" | custom-call | tf_op jit(solution)/shard_map/region_work/pallas_call | solution.py:143
  246.8 0.0 copy-start.1
  246.9 193.3 %all_to_all.22.arrived_ref = bf16[512,128,128]{2,1,0:T(8,128)(2,1)S(1)} all-to-all(bf16[512,128,128]{2,1,0:T(8,128)(2,1)} %get-tuple-element.14), channel_id=1, replica_groups=mesh['row'=8,'col'=16] {'row','col'}, dimensions={0} | all-to-all | bytes 33554432 | tf_op jit(solution)/shard_map/all_to_all | solution.py:205
  440.1 0.0 copy-done.1
  440.1 12.2 %collect_tiles.1 = f32[128,128,128]{2,1,0:T(8,128)} custom-call(s32[512]{0:T(512)S(1)} %copy-done.1, bf16[512,128,128]{2,1,0:T(8,128)(2,1)S(1)} %all_to_all.22.arrived_ref), custom_call_target="tpu_custom_call" | custom-call | tf_op jit(solution)/shard_map/collect_tiles/pallas_call | solution.py:163
Async XLA Ops:
  3.0 21.2 %all-to-all-start = ((s32[128,1,128]{2,1,0:T(1,128)}), s32[128,1,128]{2,1,0:T(1,128)S(1)}, u32[]{:S(2)}, u32[]{:S(2)}) async-start(s32[128,1,128]{2,1,0:T(1,128)} %bitcast.3), calls=%async_computation | async-start | bytes 131072 | tf_op jit(solution)/shard_map/all_to_all | solution.py:199
  24.2 0.6 copy-start.2
  33.4 191.7 %copy-start = (bf16[1,1024,2048]{2,1,0:T(8,128)(2,1)S(1)}, bf16[1,1024,2048]{2,1,0:T(8,128)(2,1)}, u32[]{:S(2)}) copy-start(bf16[1,1024,2048]{2,1,0:T(8,128)(2,1)} %param.4) | copy-start | bytes 12582916
  246.8 193.3 %copy-start.1 = (s32[512]{0:T(512)S(1)}, s32[512]{0:T(512)}, u32[]{:S(2)}) copy-start(s32[512]{0:T(512)} %get-tuple-element.11.asked_ref) | copy-start | bytes 6148
